TPU v7x, 128 devices: a whole 4x4x4 slice. The times are simulated.
128 devices in a mesh: text: 4 (over z_lo, core), img: 32 (over z_hi, x, y).
Axes of the slice: x: 4, y: 4, z: 4 (z_hi: 2, z_lo: 2; z = z_hi * 2 + z_lo), core: 2. Of those that a mesh axis runs over, the one named last changes fastest.
Arguments:
- text_in: bfloat16 [8192, 8192], P('img'), may hold values from -6 to 6
- w_query: bfloat16 [8192, 4096], P(None, 'text'), may hold values from -0.0625 to 0.0625
- gate: float32 [4096], P('text'), may hold values from -1.5 to 1.5
- image_keys: bfloat16 [2048, 4096], P('img', 'text'), may hold values from -320 to 320
- image_values: bfloat16 [2048, 4096], P('img', 'text'), may hold values from -6 to 6
- image_owner: int32 [2048], P('img'), may hold values from 0 to 7, as said below
- text_image: int32 [8192], P('img'), may hold values from 0 to 7
- cotangent: bfloat16 [8192, 4096], P('img', 'text'), may hold values from -6 to 6
Outputs:
- attended: bfloat16 [8192, 4096], P('img', 'text')
- input_grad: bfloat16 [8192, 8192], P('img', 'text')
- query_weight_grad: float32 [8192, 4096], P('img', 'text')
- gate_grad: float32 [4096], P('text')
Inputs may be any that keep to these rules, and one draw needn't show every extreme that they name: `image_owner`: image tokens of one image form one contiguous run in increasing image order; every image has a token; the largest image has exactly 512 tokens.
All inputs are finite; a program needn't handle non-finite values.
Results may differ from a plain program's by a relative error of at most 0.03.
The roundings to bfloat16 on the way count: a program that leaves them out, or rounds other values in their place, can miss the bound.
Values may be sent and summed in bfloat16 or wider, within the bound.
No kernel may reach another device: no remote copies, remote signals or barrier semaphores. Data moves between devices by JAX's collectives and lax.ppermute only.
A program may use at most 128 MiB of HBM per device.

v0:
```python
import math

import jax
import jax.numpy as jnp
from jax import lax
from jax.sharding import PartitionSpec as P

HEAD_DIM = 128


EPS = 1e-06
NEG = -1e30


def on_device(text_in, w_query, gate, image_keys, image_values, image_owner, text_image, cotangent):
    rows = text_in.shape[0]
    width = text_in.shape[1]
    channels = w_query.shape[1]
    groups = channels // HEAD_DIM
    scale = 1.0 / math.sqrt(HEAD_DIM)
    text_float = text_in.astype(jnp.float32)
    inverse_rms = lax.rsqrt(jnp.mean(text_float * text_float, axis=1, keepdims=True) + EPS)
    normed = text_float * inverse_rms
    normed_bf = normed.astype(jnp.bfloat16)
    query = (
        jnp.dot(normed_bf, w_query, preferred_element_type=jnp.float32)
        .astype(jnp.bfloat16)
        .reshape(rows, groups, HEAD_DIM)
    )

    def masked_scores(pieces):
        keys_piece, values_piece, owner_piece = pieces
        count = keys_piece.shape[0]
        keys_heads = keys_piece.reshape(count, groups, HEAD_DIM)
        values_heads = values_piece.reshape(count, groups, HEAD_DIM)
        scores = (
            jnp.einsum("khd,qhd->hkq", keys_heads, query, preferred_element_type=jnp.float32)
            * scale
        )
        allowed = (owner_piece[:, None] == text_image[None, :])[None]
        return (jnp.where(allowed, scores, NEG), allowed, keys_heads, values_heads)

    forward_peak = jnp.full((groups, rows), NEG, jnp.float32)
    scores, allowed, keys_heads, values_heads = masked_scores(
        (
            lax.all_gather(image_keys, "img", axis=0, tiled=True),
            lax.all_gather(image_values, "img", axis=0, tiled=True),
            lax.all_gather(image_owner, "img", axis=0, tiled=True),
        )
    )
    new_peak = jnp.maximum(forward_peak, jnp.max(scores, axis=1))
    weights = jnp.where(allowed, jnp.exp(scores - new_peak[:, None, :]), 0.0)
    forward_total = jnp.sum(weights, axis=1)
    accum = jnp.einsum(
        "hkq,khd->hqd",
        weights.astype(jnp.bfloat16),
        values_heads,
        preferred_element_type=jnp.float32,
    )
    peak, total, accum = (new_peak, forward_total, accum)
    attn_heads = accum / total[:, :, None]
    attn_rows = attn_heads.transpose(1, 0, 2).reshape(rows, channels)
    gate_tanh = jnp.tanh(gate)
    attended = (gate_tanh[None, :] * attn_rows).astype(jnp.bfloat16)
    upstream = cotangent.astype(jnp.float32)
    gate_grad = lax.psum(
        jnp.sum(upstream * attn_rows, axis=0) * (1.0 - gate_tanh * gate_tanh), "img"
    )
    out_grad = upstream * gate_tanh[None, :]
    out_grad_bf = out_grad.astype(jnp.bfloat16).reshape(rows, groups, HEAD_DIM)
    row_delta = jnp.sum(
        out_grad.reshape(rows, groups, HEAD_DIM).transpose(1, 0, 2) * attn_heads, axis=2
    )
    scores, allowed, keys_heads, values_heads = masked_scores(
        (
            lax.all_gather(image_keys, "img", axis=0, tiled=True),
            lax.all_gather(image_values, "img", axis=0, tiled=True),
            lax.all_gather(image_owner, "img", axis=0, tiled=True),
        )
    )
    probs = jnp.where(allowed, jnp.exp(scores - peak[:, None, :]) / total[:, None, :], 0.0)
    dprob = jnp.einsum(
        "qhd,khd->hkq", out_grad_bf, values_heads, preferred_element_type=jnp.float32
    )
    dscore = (probs * (dprob - row_delta[:, None, :])).astype(jnp.bfloat16)
    grad = jnp.einsum("hkq,khd->hqd", dscore, keys_heads, preferred_element_type=jnp.float32)
    query_grad = (grad * scale).transpose(1, 0, 2).reshape(rows, channels).astype(jnp.bfloat16)
    query_weight_grad = lax.psum_scatter(
        lax.dot_general(
            normed_bf, query_grad, (((0,), (0,)), ((), ())), preferred_element_type=jnp.float32
        ).astype(jnp.bfloat16),
        "img",
        scatter_dimension=0,
        tiled=True,
    ).astype(jnp.float32)
    partial_grad = lax.dot_general(
        query_grad, w_query, (((1,), (1,)), ((), ())), preferred_element_type=jnp.float32
    )
    share = width // lax.axis_size("text")
    offset = lax.axis_index("text") * share
    normed_share = lax.dynamic_slice_in_dim(normed, offset, share, 1)
    normed_grad = lax.psum(partial_grad, "text")
    row_mean = jnp.mean(normed_grad * normed, axis=1, keepdims=True)
    grad_share = lax.dynamic_slice_in_dim(normed_grad, offset, share, 1)
    input_grad = (inverse_rms * (grad_share - normed_share * row_mean)).astype(jnp.bfloat16)
    return (attended, input_grad, query_weight_grad, gate_grad)


def solution(mesh):
    in_specs = (
        P("img", None),
        P(None, "text"),
        P("text"),
        P("img", "text"),
        P("img", "text"),
        P("img"),
        P("img"),
        P("img", "text"),
    )
    out_specs = (P("img", "text"), P("img", "text"), P("img", "text"), P("text"))
    return jax.shard_map(
        on_device, mesh=mesh, in_specs=in_specs, out_specs=out_specs, check_vma=False
    )
```

profile of v0, /device:TPU:0, one launch (start us, length us, event | category | flops | bytes accessed | tf_op | source)
XLA Modules:
  0.0 625.7 jit_solution(6353246872428662665)
XLA Ops:
  7.2 0.7 all-gather.3.cloned.1.call-update
  7.9 0.7 all-gather.5.cloned.1.call-update
  8.7 0.7 tanh.3
  9.4 1.2 dynamic-slice
  11.3 0.9 dynamic-update-slice
  12.2 22.3 %all-reduce = s32[2048]{0:T(1024)S(1)} all-reduce(s32[2048]{0:T(1024)S(1)} %dynamic-update-slice), channel_id=1, replica_groups=mesh['text'=4,'img'=32] {'img'}, use_global_device_ids=true, to_apply=%add | all-reduce | flops 2048 | bytes 16384
  34.5 3.1 fusion.2
  37.6 1.0 broadcast_compare_fusion
  38.6 11.7 %fusion.21 = bf16[32,8,8,128]{3,2,1,0:T(8,128)(2,1)S(1)} fusion(bf16[8192,1024]{1,0:T(8,128)(2,1)} %param.9, bf16[256,8192]{1,0:T(8,128)(2,1)} %param.8, f32[256]{0:T(256)S(1)} %add_rsqrt_fusion), kind=kOutput, calls=%fused_computation.25 | convolution fusion | flops 4301520896 | bytes 21496832 | tf_op jit(solution)/shard_map/dot_general | solution.py:26
  50.4 45.8 %all-gather.3.cloned.1.call-done = bf16[2048,1024]{1,0:T(8,128)(2,1)} async-done(((bf16[64,1024]{1,0:T(8,128)(2,1)}), bf16[2048,1024]{1,0:T(8,128)(2,1)}) %all-gather.3.cloned.1.call-update) | async-done | bytes 4194320 | tf_op jit(solution)/shard_map/all_gather | solution.py:46
  96.2 6.5 %copy.29 = bf16[2048,1024]{0,1:T(8,128)(2,1)} copy(bf16[2048,1024]{1,0:T(8,128)(2,1)} %all-gather.3.cloned.1.call-done) | data formatting | bytes 8388608 | tf_op jit(solution)/shard_map/all_gather | solution.py:46
  102.7 5.3 fusion.1
  108.0 5.7 copy-done
  113.7 5.0 select_reduce_fusion
  118.7 59.9 %all-gather.5.cloned.1.call-done = bf16[2048,1024]{1,0:T(8,128)(2,1)} async-done(((bf16[64,1024]{1,0:T(8,128)(2,1)}), bf16[2048,1024]{1,0:T(8,128)(2,1)}) %all-gather.5.cloned.1.call-update) | async-done | bytes 4194320 | tf_op jit(solution)/shard_map/all_gather | solution.py:47
  178.6 6.5 %copy.32 = bf16[2048,1024]{0,1:T(8,128)(2,1)} copy(bf16[2048,1024]{1,0:T(8,128)(2,1)} %all-gather.5.cloned.1.call-done) | data formatting | bytes 8388608 | tf_op jit(solution)/shard_map/all_gather | solution.py:47
  185.0 10.6 %bitcast_divide_fusion = (f32[256,8,128]{0,2,1:T(8,128)S(1)}, f32[8,256,128]{1,2,0:T(8,128)}) fusion(f32[256,8]{0,1:T(8,128)S(1)} %bitcast.71, bf16[2048,8,128]{0,2,1:T(8,128)(2,1)} %bitcast.66, f32[8,256,2048]{2,1,0:T(8,128)} %copy-done, f32[8,256]{1,0:T(8,128)S(1)} %broadcast_maximum_fusion, pred[2048,256]{0,1:T(8,128)(4,1)S(1)} %broadcast_compare_fusion), kind=kOutput, calls=%fused_computation.27 | convolution fusion | flops 1094975488 | bytes 23609344 | tf_op jit(solution)/shard_map/hkq,khd->hqd/dot_general | solution.py:54
  195.6 0.3 copy.34
  196.0 1.3 fusion.24
  197.3 0.3 copy.37
  197.6 1.4 multiply_reduce_fusion.1
  199.0 13.9 %fusion.15 = bf16[8,256,128]{1,2,0:T(8,128)(2,1)S(1)} fusion(bf16[2048,8,128]{0,2,1:T(8,128)(2,1)} %bitcast.65, f32[8,256,2048]{2,1,0:T(8,128)} %copy-done, f32[8,256]{1,0:T(8,128)S(1)} %multiply_reduce_fusion.1, f32[8,256]{1,0:T(8,128)S(1)} %select_reduce_fusion, f32[8,256]{1,0:T(8,128)S(1)} %broadcast_maximum_fusion, ...), kind=kOutput, calls=%fused_computation.23 | convolution fusion | flops 2181562368 | bytes 26763264 | tf_op jit(solution)/shard_map/hkq,khd->hqd/dot_general | solution.py:86
  212.9 19.3 %fusion.38 = f32[256,8192]{1,0:T(8,128)} fusion(bf16[256,1024]{0,1:T(8,128)(2,1)S(1)} %bitcast.68, bf16[8192,1024]{1,0:T(8,128)(2,1)} %param.9), kind=kOutput, calls=%fused_computation.47 | convolution fusion | flops 4294967296 | bytes 25690112 | tf_op jit(solution)/shard_map/dot_general | solution.py:96
  232.2 0.0 reduce-scatter.2.cloned.1.call-start
  232.2 10.8 %convolution_convert_fusion = bf16[8192,1024]{1,0:T(8,128)(2,1)} fusion(bf16[256,1024]{0,1:T(8,128)(2,1)S(1)} %bitcast.69, bf16[256,8192]{1,0:T(8,128)(2,1)} %param.8, f32[256]{0:T(256)S(1)} %add_rsqrt_fusion), kind=kOutput, calls=%fused_computation.6 | convolution fusion | flops 4309647360 | bytes 21496832 | tf_op jit(solution)/shard_map/dot_general | solution.py:89
  243.0 0.7 copy-done.2
  243.7 93.4 %psum.15 = f32[1024]{0:T(1024)} all-reduce(f32[1024]{0:T(1024)S(1)} %subtract_multiply_fusion), channel_id=1, replica_groups=mesh['text'=4,'img'=32] {'img'}, use_global_device_ids=true, to_apply=%region_8.9 | all-reduce | flops 1024 | bytes 8192 | tf_op jit(solution)/shard_map/psum | solution.py:66
  337.1 51.6 %all-reduce.3.cloned.1.call-done = f32[256,8192]{1,0:T(8,128)} async-done(((f32[256,8192]{1,0:T(8,128)}), f32[256,8192]{1,0:T(8,128)}) %all-reduce.3.cloned.1.call-update) | async-done | bytes 8388624 | tf_op jit(solution)/shard_map/psum | solution.py:102
  388.6 5.8 multiply_reduce_fusion
  394.5 3.0 multiply_convert_fusion
  397.4 219.6 %reduce-scatter.2.cloned.1.call-done = bf16[256,1024]{1,0:T(8,128)(2,1)} async-done(((bf16[8192,1024]{1,0:T(8,128)(2,1)}), bf16[256,1024]{1,0:T(8,128)(2,1)}) %reduce-scatter.2.cloned.1.call-update) | async-done | bytes 524304 | tf_op jit(solution)/shard_map/reduce_scatter | solution.py:88
  617.1 2.1 convert_element_type.55
  (14 shorter events, 0.2 us)
Async XLA Ops:
  7.2 89.0 %all-gather.3.cloned.1.call-start = ((), (), s32[]{:S(2)}) async-start(), calls=%async_computation.1 | async-start | bytes 4325376 | tf_op jit(solution)/shard_map/all_gather | solution.py:46
  7.9 170.7 %all-gather.5.cloned.1.call-start = ((), (), s32[]{:S(2)}) async-start(), calls=%async_computation.2 | async-start | bytes 4325376 | tf_op jit(solution)/shard_map/all_gather | solution.py:47
  8.6 380.0 %all-reduce.3.cloned.1.call-start = ((), (), s32[]{:S(2)}) async-start(), calls=%async_computation.3 | async-start | bytes 16777216 | tf_op jit(solution)/shard_map/psum | solution.py:102
  107.9 5.7 copy-start
  185.0 11.0 %copy-start.1 = (bf16[256,1024]{1,0:T(8,128)(2,1)S(1)}, bf16[256,1024]{1,0:T(8,128)(2,1)}, u32[]{:S(2)}) copy-start(bf16[256,1024]{1,0:T(8,128)(2,1)} %param.15) | copy-start | bytes 1572868
  232.2 384.9 %reduce-scatter.2.cloned.1.call-start = ((), (), s32[]{:S(2)}) async-start(), calls=%async_computation.4 | async-start | bytes 17301504 | tf_op jit(solution)/shard_map/reduce_scatter | solution.py:88
  243.0 0.7 copy-start.2
Sparse Core Ops, SparseCore 0:
  11.1 85.0 all-gather.2
  99.2 79.2 all-gather.4
  232.3 156.2 all-reduce.2
  390.9 226.1 reduce-scatter.1
where the time goes:
time: 626 us
  waiting for transfers between devices  378 us (60%)
  blocking collectives  116 us (19%)
  matrix products  71.5 us (11%)
  local copies, waits for them, and re-layouts  22.8 us (4%)
  other arithmetic  22.8 us (4%)
  between operations  14.5 us (2%)
    reduce_scatter x1, waiting for transfers between devices, on_device(): lax.psum_scatter(lax.dot_general(normed_bf, query_grad, (((0,), (0,)), ((...  220 us
    psum x1, blocking collectives, on_device(): lax.psum(jnp.sum(upstream * attn_rows, axis=0) * (1.0 - gate_tanh * gate_...  93.4 us
    all_gather x1, waiting for transfers between devices, on_device(): lax.all_gather(image_values, 'img', axis=0, tiled=True)  59.9 us
    psum x1, waiting for transfers between devices, on_device(): normed_grad = lax.psum(partial_grad, 'text')  51.6 us
    all_gather x1, waiting for transfers between devices, on_device(): lax.all_gather(image_keys, 'img', axis=0, tiled=True)  45.8 us
    unnamed x1, blocking collectives  22.3 us
    dot_general x1, matrix products, on_device(): lax.dot_general(query_grad, w_query, (((1,), (1,)), ((), ())), preferred_...  19.3 us
    dot_general x1, matrix products, on_device(): jnp.einsum('hkq,khd->hqd', dscore, keys_heads, preferred_element_type=jnp...  13.9 us
  transfers between devices with their start and end apart: 4, of which 4 were waited for; matrix products, arithmetic and copies ran while one was open for 9% of the time, Pallas kernels for 0%

commit v1 on v0

v1 whole, which is shorter than its diff:
```python
import functools
import math

import jax
import jax.numpy as jnp
from jax import lax
from jax.experimental import pallas as pl
from jax.experimental.pallas import tpu as pltpu
from jax.sharding import PartitionSpec as P

HEAD_DIM = 128
EPS = 1e-06
NEG = -1e30
SCALE = 1.0 / math.sqrt(HEAD_DIM)
BF16 = jnp.bfloat16
F32 = jnp.float32

STEP = {"x": 4, "y": 1}
AXES = (("x", "y"), ("y", "x"))
Z, X, Y, Z_LO, CORE = range(5)


def moved(i, axis, r):
    step = STEP[axis]
    at = (i // step) % 4
    return i + (((at + r) % 4) - at) * step


def pull(value, axis, r):
    return lax.ppermute(value, "img", [(i, moved(i, axis, -r)) for i in range(32)])


def pull_z(value):
    return lax.ppermute(value, "img", [(i, i ^ 16) for i in range(32)])


def pull_text(value, bit):
    return lax.ppermute(value, "text", [(i, i ^ bit) for i in range(4)])


def call(body, pos, inputs, outs, in_specs=None, out_specs=None, grid=(1,), scratch=(), after=(), us=0.6, vmem=24):
    def whole(shape):
        return pl.BlockSpec(shape, lambda i, pos: (0,) * len(shape))

    in_specs = list(in_specs) if in_specs else [None] * len(inputs)
    out_specs = list(out_specs) if out_specs else [None] * len(outs)
    in_specs = [s or whole(v.shape) for s, v in zip(in_specs, inputs)]
    out_specs = [s or whole(v.shape) for s, v in zip(out_specs, outs)]
    count = 1 + len(inputs)

    def kernel(*refs):
        body(*refs[:count], *refs[count + len(after):])

    return pl.pallas_call(
        kernel,
        grid_spec=pltpu.PrefetchScalarGridSpec(
            num_scalar_prefetch=1,
            grid=grid,
            in_specs=in_specs + [pl.BlockSpec(memory_space=pl.ANY)] * len(after),
            out_specs=out_specs,
            scratch_shapes=list(scratch),
        ),
        out_shape=list(outs),
        compiler_params=pltpu.CompilerParams(vmem_limit_bytes=vmem * 1024 * 1024),
        cost_estimate=pl.CostEstimate(flops=int(us * 1.0e9), bytes_accessed=int(us * 3.0e6), transcendentals=0),
    )(pos, *inputs, *after)


def like(shape, dtype=BF16):
    return jax.ShapeDtypeStruct(shape, dtype)


def lanes(start, size):
    return pl.ds(pl.multiple_of(start, 128), size)


def sum_parts(rows):
    rows = rows.astype(F32)
    return rows[0:1] + rows[1:2] + rows[2:3]


def three_parts(value):
    high = value.astype(BF16).astype(F32)
    middle = (value - high).astype(BF16).astype(F32)
    return [high, middle, value - high - middle]


def pack_body(pos, k_ref, v_ref, cot_ref, extra_ref, *outs):
    for s in range(2):
        at = pos[X + s]
        for r in range(4):
            column = s * 512 + ((at + 4 - r) % 4) * 128
            out = outs[s * 4 + r]
            out[0:64] = k_ref[:, lanes(column, 128)]
            out[64:128] = v_ref[:, lanes(column, 128)]
            out[128:144] = extra_ref[0:16]
            out[144:400] = cot_ref[:, lanes(column, 128)]
            out[400:416] = extra_ref[16:32]


def near_body(pos, *refs):
    for r in range(8):
        refs[8][r] = refs[r][...]


def merge_body(pos, near_ref, far_ref, *refs):
    count = len(refs) // 2
    refs[count][0:4] = near_ref[...]
    refs[count][4:8] = far_ref[...]
    for n in range(count):
        refs[count + 1 + n][...] = refs[n][...]


def copy_body(pos, *refs):
    count = len(refs) // 2
    for r in range(count):
        refs[count + r][...] = refs[r][...]


def stack_body(pos, *refs):
    for r in range(3):
        refs[3][r] = refs[r][...]


def norm_body(pos, x_ref, normed_ref, inverse_ref):
    x = x_ref[...].astype(F32)
    inverse = lax.rsqrt(jnp.mean(x * x, axis=1, keepdims=True) + EPS)
    inverse_ref[...] = jnp.broadcast_to(inverse, inverse_ref.shape)
    normed_ref[...] = (x * inverse).astype(BF16)


def query_body(pos, normed_ref, w0, w1, w2, w3, query_ref):
    step = pl.program_id(0)
    part = None
    for n, w_ref in enumerate((w0, w1, w2, w3)):
        term = jnp.dot(normed_ref[:, n * 256:(n + 1) * 256], w_ref[...], preferred_element_type=F32)
        part = term if part is None else part + term

    @pl.when(step == 0)
    def _():
        query_ref[...] = part

    @pl.when(step != 0)
    def _():
        query_ref[...] += part


def chunks_body(pos, query_ref, *outs):
    for s in range(2):
        for r in range(4):
            column = s * 512 + ((pos[X + s] + 4 - r) % 4) * 128
            outs[s * 4 + r][...] = query_ref[:, lanes(column, 128)].astype(BF16)


def attention_body(s, pos, *refs):
    queries, messages, quarters = refs[0:4], refs[4:8], refs[8:12]
    gate_ref, out_refs = refs[12], refs[13:17]
    q_s, cot_s, image_s, att_s, grad_ref, s_ref = refs[17:]
    pieces = [q.at[h * 4:h * 4 + 4] for q in quarters for h in range(2)]
    for r in range(4):
        q_s[r] = queries[r][...]
        cot_s[r] = messages[r][144:400]
        image_s[r] = messages[r][400:416]
    tanh = jnp.tanh(gate_ref[:, lanes(s * 512 + pos[X + s] * 128, 128)])

    def keys(i):
        return pieces[i][:, 0:64, :].reshape(256, HEAD_DIM)

    def values(i):
        return pieces[i][:, 64:128, :].reshape(256, HEAD_DIM)

    owners = []
    for i in range(8):
        for j in (0, 2):
            left = pieces[i][j, 128:144, :].astype(F32)
            right = pieces[i][j + 1, 128:144, :].astype(F32)
            owners.append(left[0:1] + right[1:2])

    def block(t, gate_sum):
        query = q_s[t]
        rows = image_s[t].astype(F32)
        image = jnp.concatenate(
            [jnp.transpose(jnp.broadcast_to(rows[h:h + 1], (128, 128))) for h in range(2)], 0
        )
        top = jnp.full((256, 128), NEG, F32)
        for i in range(8):
            sc = lax.dot_general(query, keys(i), (((1,), (1,)), ((), ())), preferred_element_type=F32)
            for h in range(2):
                part = jnp.where(image == owners[2 * i + h], sc[:, h * 128:(h + 1) * 128], NEG)
                s_ref[:, i * 256 + h * 128:i * 256 + (h + 1) * 128] = part
                top = jnp.maximum(top, part)
        peak = jnp.max(top, axis=1, keepdims=True)
        total = jnp.zeros((256, 128), F32)
        accum = jnp.zeros((256, HEAD_DIM), F32)
        for i in range(8):
            w = jnp.exp((s_ref[:, i * 256:(i + 1) * 256] - peak) * SCALE)
            s_ref[:, i * 256:(i + 1) * 256] = w
            total = total + (w[:, :128] + w[:, 128:])
            accum = accum + jnp.dot(w.astype(BF16), values(i), preferred_element_type=F32)
        inverse = 1.0 / jnp.sum(total, axis=1, keepdims=True)
        attn = accum * inverse
        upstream = cot_s[t].astype(F32)
        att_s[t] = (attn * tanh).astype(BF16)
        out_grad = upstream * tanh
        delta = jnp.sum(out_grad * attn, axis=1, keepdims=True)
        out_grad = out_grad.astype(BF16)
        grad = jnp.zeros((256, HEAD_DIM), F32)
        for i in range(8):
            dprob = lax.dot_general(out_grad, values(i), (((1,), (1,)), ((), ())), preferred_element_type=F32)
            dscore = ((s_ref[:, i * 256:(i + 1) * 256] * inverse) * (dprob - delta)).astype(BF16)
            grad = grad + jnp.dot(dscore, keys(i), preferred_element_type=F32)
        grad_ref[pl.ds(pl.multiple_of(t * 256, 256), 256)] = (grad * SCALE).astype(BF16)
        return gate_sum + jnp.sum(upstream * attn, axis=0, keepdims=True)

    gate_sum = lax.fori_loop(0, 4, block, jnp.zeros((1, HEAD_DIM), F32))
    grad_ref[1024:1040] = jnp.concatenate(three_parts(gate_sum) + [jnp.zeros((13, 128), F32)], 0).astype(BF16)
    for r in range(4):
        out_refs[r][0:1040] = grad_ref[...]
        out_refs[r][1040:1296] = att_s[(4 - r) % 4]


def product(half, b, parts):
    out = None
    for j in range(4):
        term = lax.dot_general(
            parts(half, j), b[j * 256:(j + 1) * 256], (((0,), (0,)), ((), ())), preferred_element_type=F32
        )
        out = term if out is None else out + term
    return out


def parts_of(refs):
    def part(half, j):
        if j == 0:
            return refs[half][...]
        return refs[5][j - 1] if half else refs[1 + j][...]

    return part


def first_body(s, pos, *refs):
    messages, part = refs[0:4], parts_of(refs[4:10])
    out_refs, keep_ref, gate_ref, b_ref = refs[10:13], refs[13], refs[14], refs[15]
    step = pl.program_id(0)

    @pl.when(step == 0)
    def _():
        for r in range(4):
            column = ((pos[X + s] + r) % 4) * 128
            for j in range(4):
                source = ((j - r) % 4) * 256
                b_ref[j * 256:(j + 1) * 256, lanes(column, 128)] = messages[r][source:source + 256]
            gate_ref[:, lanes(column, 128)] = sum_parts(messages[r][1024:1040])
        rows = jnp.concatenate(three_parts(gate_ref[...]) + [jnp.zeros((13, 512), F32)], 0).astype(BF16)
        for out_ref in out_refs:
            out_ref[512:528] = rows

    for half in range(2):
        rows = slice(half * 256, (half + 1) * 256)
        acc = product(half, b_ref, part)
        for n, out_ref in enumerate(out_refs):

            @pl.when(step == n)
            def _():
                out_ref[rows] = acc.astype(BF16)

        @pl.when(step == 3)
        def _():
            keep_ref[rows] = acc


def third_body(pos, *refs):
    keep_in, gate_ref, got = refs[0], refs[1], refs[2:5]
    send_ref, keep_ref, gate_out, total = refs[5:]
    for half in range(2):
        rows = slice(half * 256, (half + 1) * 256)
        total[half] = keep_in[rows] + (got[0][rows].astype(F32) + got[1][rows].astype(F32) + got[2][rows].astype(F32))
    keep = (pos[Z] + pos[CORE]) % 2
    send_ref[0:256] = total[1 - keep].astype(BF16)
    keep_ref[...] = total[keep]
    gate = gate_ref[...]
    for ref in got:
        gate = gate + sum_parts(ref[512:528])
    gate_out[...] = gate
    send_ref[256:272] = jnp.concatenate(three_parts(gate) + [jnp.zeros((13, 512), F32)], 0).astype(BF16)


def last_body(pos, *refs):
    gate_ref, out_ref, grad_ref = refs[0], refs[7], refs[8]
    tanh = jnp.tanh(gate_ref[...])
    for s in range(2):
        keep_ref, sum_ref, got_ref = refs[1 + 3 * s:4 + 3 * s]
        columns = slice(s * 512, (s + 1) * 512)
        out_ref[:, columns] = keep_ref[...] + got_ref[0:256].astype(F32)
        t = tanh[:, columns]
        grad_ref[:, columns] = (sum_ref[...] + sum_parts(got_ref[256:272])) * (1.0 - t * t)


def partial_grad(grad, w_refs):
    dims = (((1,), (1,)), ((), ()))
    return jnp.concatenate(
        [lax.dot_general(grad, w_ref[...], dims, preferred_element_type=F32) for w_ref in w_refs], 1
    )


def input_first_body(pos, *refs):
    messages = refs[0:8]
    query_ref, inverse_ref, x_ref, w0, w1, w2, w3, send_ref, share_ref, grad_ref = refs[8:]

    @pl.when(pl.program_id(0) == 0)
    def _():
        for s in range(2):
            for r in range(4):
                column = s * 512 + ((pos[X + s] + r) % 4) * 128
                source = ((4 - r) % 4) * 256
                grad_ref[:, lanes(column, 128)] = messages[s * 4 + r][source:source + 256]
        share = jnp.sum(grad_ref[...].astype(F32) * query_ref[...], axis=1, keepdims=True)
        share_ref[...] = jnp.broadcast_to(share * (1.0 / 8192.0), share_ref.shape)

    h = x_ref[...].astype(F32) * inverse_ref[:, :1]
    send_ref[...] = (partial_grad(grad_ref[...], (w0, w1, w2, w3)) - h * share_ref[:, :1]).astype(BF16)


def input_next_body(pos, grad_ref, share_ref, inverse_ref, x_ref, w0, w1, w2, w3, got_ref, out_ref):
    h = x_ref[...].astype(F32) * inverse_ref[:, :1]
    out = partial_grad(grad_ref[...], (w0, w1, w2, w3)) - h * share_ref[:, :1] + got_ref[...].astype(F32)
    out_ref[...] = out.astype(out_ref.dtype)


def input_last_body(pos, keep_ref, got_ref, inverse_ref, out_ref):
    out_ref[...] = ((keep_ref[...] + got_ref[...].astype(F32)) * inverse_ref[:, :1]).astype(BF16)


def home_body(pos, *refs):
    out_ref = refs[8]
    for s in range(2):
        for r in range(4):
            column = s * 512 + ((pos[X + s] + r) % 4) * 128
            out_ref[:, lanes(column, 128)] = refs[s * 4 + r][1040:1296]


def on_device(text_in, w_query, gate, image_keys, image_values, image_owner, text_image, cotangent):
    where, member = lax.axis_index("img"), lax.axis_index("text")
    pos = jnp.stack([where // 16, (where // 4) % 4, where % 4, member // 2, member % 2]).astype(jnp.int32)
    gate_row = gate.reshape(1, 1024)

    owner = image_owner.astype(BF16)
    empty = jnp.zeros((64,), BF16)
    pair = jnp.stack([jnp.concatenate([owner, empty]), jnp.concatenate([empty, owner])])
    extra = jnp.concatenate([jnp.tile(pair, (8, 1)), jnp.tile(text_image.astype(BF16).reshape(2, 128), (8, 1))], 0)
    packed = call(pack_body, pos, [image_keys, image_values, cotangent, extra], [like((416, 128))] * 8)
    first = []
    for s, (axis, other) in enumerate(AXES):
        mine = packed[s * 4:s * 4 + 4]
        first.append([mine[0]] + [pull(mine[r], axis, r) for r in (1, 2, 3)])
    rows = lambda width: pl.BlockSpec((32, width), lambda i, pos: (i, 0))
    normed, inverse = call(
        norm_body, pos, [text_in], [like((256, 8192)), like((256, 128), F32)],
        in_specs=[rows(8192)], out_specs=[rows(8192), rows(128)], grid=(8,), after=[packed[0]], us=2.6,
    )
    kv_rows = pl.BlockSpec((144, 128), lambda i, pos: (0, 0))
    near = call(near_body, pos, first[0] + first[1], [like((8, 144, 128))], in_specs=[kv_rows] * 8)[0]
    far = pull_z(near)

    def cut(s, backs, after):
        if s == 0:
            block = lambda r: pl.BlockSpec((256, 1024), lambda i, pos: (0, pos[CORE] * 4 + (pos[X] + 4 - r) % 4))
            out = pl.BlockSpec((256, 1024), lambda i, pos: (0, 0))
        else:
            block = lambda r: pl.BlockSpec(
                (256, 256), lambda i, pos: (0, pos[CORE] * 16 + i * 4 + (pos[Y] + 4 - r) % 4)
            )
            out = pl.BlockSpec((256, 256), lambda i, pos: (0, i))
        return call(
            copy_body, pos, [normed] * len(backs), [like((256, 1024))] * len(backs),
            in_specs=[block(r) for r in backs], out_specs=[out] * len(backs), grid=(1 + 3 * s,), after=after,
        )

    def stack(got, after=()):
        return call(stack_body, pos, got, [like((3, 256, 1024))], after=after)[0]

    quarter = lambda s: pl.BlockSpec((4, 144, 128), lambda i, pos: (s, 0, 0))

    def merge(s, others, after):
        mine, *rest = call(
            merge_body, pos, [near, far] + others, [like((8, 144, 128))] + [like((256, 128))] * len(others),
            in_specs=[quarter(s)] * 2 + [None] * len(others), after=after,
        )
        return [mine] + [pull(mine, AXES[s][1], r) for r in (1, 2, 3)], rest

    def attend(s, after):
        return call(
            functools.partial(attention_body, s), pos, queries[s] + first[s] + quarters[s] + [gate_row],
            [like((1296, 128))] * 4,
            scratch=[
                pltpu.VMEM((4, 256, 128), BF16),
                pltpu.VMEM((4, 256, 128), BF16),
                pltpu.VMEM((4, 16, 128), BF16),
                pltpu.VMEM((4, 256, 128), BF16),
                pltpu.VMEM((1040, 128), BF16),
                pltpu.VMEM((256, 2048), F32),
            ],
            after=after, us=8.5,
        )

    early = cut(0, (1, 3), [near])
    got_x = [pull(early[0], "x", 1), None, pull(early[1], "x", 3)]
    quarters = [merge(0, [], [early[0]])[0]]
    early = cut(0, (2,), [got_x[0], got_x[2]])
    got_x[1] = pull(early[0], "x", 2)
    query = call(
        query_body, pos, [normed] + [w_query] * 4,
        [like((256, 1024), F32)],
        in_specs=[
            pl.BlockSpec((256, 1024), lambda i, pos: (0, i)),
        ] + [pl.BlockSpec((256, 1024), lambda i, pos, n=n: (i * 4 + n, 0)) for n in range(4)],
        grid=(8,), after=[quarters[0][0], early[0]], us=11.0, vmem=48,
    )[0]
    chunks = call(chunks_body, pos, [query], [like((256, 128))] * 8, after=quarters[0][1:] + [got_x[1]])
    swapped = [pull_text(stack(got_x, [chunks[0]]), 1)]
    queries = [
        [chunks[s * 4]] + [pull(chunks[s * 4 + r], axis, r) for r in (1, 2, 3)] for s, (axis, other) in enumerate(AXES)
    ]
    quarters.append(merge(1, [], queries[0][1:] + queries[1][1:] + swapped)[0])
    late = cut(1, (1, 3, 2), [quarters[1][0]])
    results = [attend(0, late)]
    results.append(attend(1, [results[0][0]]))
    got_y = [pull(late[(0, 2, 1)[r - 1]], "y", r) for r in (1, 2, 3)]
    swapped.append(pull_text(stack(got_y, [results[1][0]]), 1))
    parts = [[normed, normed] + got + [swapped[s]] for s, got in enumerate((got_x, got_y))]

    def part_specs(s, order):
        axis = X + (1 - s)
        at = lambda i, pos: (pos[axis] + order(i)) % 4
        own = lambda i, pos: pos[X] * 4 + at(i, pos) if s == 0 else at(i, pos) * 4 + pos[Y]
        return (
            [
                pl.BlockSpec((256, 256), lambda i, pos: (0, pos[CORE] * 16 + own(i, pos))),
                pl.BlockSpec((256, 256), lambda i, pos: (0, (1 - pos[CORE]) * 16 + own(i, pos))),
            ]
            + [pl.BlockSpec((256, 256), lambda i, pos: (0, at(i, pos)))] * 3
            + [pl.BlockSpec((3, 256, 256), lambda i, pos: (0, 0, at(i, pos)))]
        )

    messages = []
    for s, (axis, other) in enumerate(AXES):
        mine = results[s]
        messages.append([mine[0]] + [pull(mine[r], axis, r) for r in (1, 2, 3)])

    def first_chunks(s, after):
        *sends, keep, gate_sum = call(
            functools.partial(first_body, s), pos, messages[s] + parts[s],
            [like((528, 512))] * 3 + [like((512, 512), F32), like((1, 512), F32)],
            in_specs=[None] * 4 + part_specs(s, lambda i: i + 1),
            scratch=[pltpu.VMEM((1024, 512), BF16)],
            grid=(4,), after=after, us=6.0,
        )
        got = [pull(v, AXES[s][1], -m) for v, m in zip(sends, (1, 2, 3))]
        return [keep, gate_sum] + got, sends[0]

    def third(s, values, after):
        message, keep, gate_total = call(
            third_body, pos, values, [like((272, 512)), like((256, 512), F32), like((1, 512), F32)],
            scratch=[pltpu.VMEM((2, 256, 512), F32)], after=after,
        )
        return [keep, gate_total, pull_z(message)]

    def column_specs(block):
        return [
            pl.BlockSpec((256, 1024), lambda i, pos: (0, block(i, pos))),
        ] + [pl.BlockSpec((256, 1024), lambda i, pos, n=n: (block(i, pos) * 4 + n, 0)) for n in range(4)]

    values0, done0 = first_chunks(0, [results[1][0]])
    send, share, grad_own = call(
        input_first_body, pos, messages[0] + messages[1] + [query, inverse, text_in] + [w_query] * 4,
        [like((256, 4096)), like((256, 128), F32), like((256, 1024))],
        in_specs=[None] * 10 + column_specs(lambda i, pos: (i // 2) * 4 + (1 - pos[CORE]) * 2 + i % 2),
        out_specs=[pl.BlockSpec((256, 1024), lambda i, pos: (0, i)), None, None],
        grid=(4,), after=[done0], us=8.0, vmem=48,
    )
    got_core = pull_text(send, 1)

    def input_next(z_of, dtype, after):
        return call(
            input_next_body, pos, [grad_own, share, inverse, text_in] + [w_query] * 4 + [got_core],
            [like((256, 2048), dtype)],
            in_specs=[None] * 3
            + column_specs(lambda i, pos: z_of(pos) * 4 + pos[CORE] * 2 + i)
            + [pl.BlockSpec((256, 1024), lambda i, pos: (0, z_of(pos) * 2 + i))],
            out_specs=[pl.BlockSpec((256, 1024), lambda i, pos: (0, i))],
            grid=(2,), after=after, us=4.0, vmem=48,
        )[0]

    values1, done1 = first_chunks(1, [send])
    send_z_lo = input_next(lambda pos: 1 - pos[Z_LO], BF16, [done1])
    closing = third(0, values0, [send_z_lo])
    got_z_lo = pull_text(send_z_lo, 2)
    keep_input = input_next(lambda pos: pos[Z_LO], F32, [closing[0]])
    attended = call(home_body, pos, messages[0] + messages[1], [like((256, 1024))], after=[keep_input])[0]
    closing += third(1, values1, [attended])
    query_weight_grad, gate_grad = call(
        last_body, pos, [gate_row] + closing, [like((256, 1024), F32), like((1, 1024), F32)], after=[closing[3]]
    )
    input_grad = call(input_last_body, pos, [keep_input, got_z_lo, inverse], [like((256, 2048))])[0]
    return (attended, input_grad, query_weight_grad, gate_grad.reshape(1024))


def solution(mesh):
    in_specs = (
        P("img", None),
        P(None, "text"),
        P("text"),
        P("img", "text"),
        P("img", "text"),
        P("img"),
        P("img"),
        P("img", "text"),
    )
    out_specs = (P("img", "text"), P("img", "text"), P("img", "text"), P("text"))
    return jax.shard_map(
        on_device, mesh=mesh, in_specs=in_specs, out_specs=out_specs, check_vma=False
    )
```

time: 626 us -> 196 us (0.31)
  waiting for transfers between devices: 378 us -> 44.6 us
  blocking collectives: 116 us -> 0 us
  Pallas kernels: 0 us -> 74.6 us
  matrix products: 71.5 us -> 0 us
  starting transfers between devices: 0.16 us -> 61.3 us
  other arithmetic: 22.8 us -> 1.36 us
  between operations: 14.5 us -> 1.11 us
  local copies, waits for them, and re-layouts: 22.8 us -> 11.5 us
    reduce_scatter x1 -> x0, waiting for transfers between devices: 220 us -> none  [on_device(): lax.psum_scatter(lax.dot_general(normed_bf, query_grad, (((0,), (0,)), ((...]
    all_gather x2 -> x0, waiting for transfers between devices: 106 us -> none  [the longest x1 59.9 us: on_device(): lax.all_gather(image_values, 'img', axis=0, tiled=True)]
    psum x1 -> x0, blocking collectives: 93.4 us -> none  [on_device(): lax.psum(jnp.sum(upstream * attn_rows, axis=0) * (1.0 - gate_tanh * gate_...]
    pallas_call x0 -> x24, Pallas kernels: none -> 74.6 us  [call(): pl.pallas_call(kernel, grid_spec=pltpu.PrefetchScalarGridSpec(num_scalar_...]
    dot_general x6 -> x0, matrix products: 71.5 us -> none  [the longest x1 19.3 us: on_device(): lax.dot_general(query_grad, w_query, (((1,), (1,)), ((), ())), preferred_...]
    ppermute x0 -> x43, starting transfers between devices: none -> 61.3 us  [the longest x36 49 us: pull(): lax.ppermute(value, 'img', [(i, moved(i, axis, -r)) for i in range(32)])]
    psum x1 -> x0, waiting for transfers between devices: 51.6 us -> none  [on_device(): normed_grad = lax.psum(partial_grad, 'text')]
    ppermute x0 -> x43, waiting for transfers between devices: none -> 44.6 us  [the longest x36 33.4 us: pull(): lax.ppermute(value, 'img', [(i, moved(i, axis, -r)) for i in range(32)])]
  transfers between devices with their start and end apart: 4 -> 43, of which waited for: 4 -> 15; matrix products, arithmetic and copies ran while one was open for 9% -> 0% of each run, Pallas kernels for 0% -> 35%
where the time goes in v1:
time: 196 us; the launch traced here: 195 us
  Pallas kernels  74.6 us (38%)
  starting transfers between devices  61.3 us (31%)
  waiting for transfers between devices  44.6 us (23%)
  local copies, waits for them, and re-layouts  11.5 us (6%)
    pallas_call x24, Pallas kernels, call(): pl.pallas_call(kernel, grid_spec=pltpu.PrefetchScalarGridSpec(num_scalar_...  74.6 us
    ppermute x36, starting transfers between devices, pull(): lax.ppermute(value, 'img', [(i, moved(i, axis, -r)) for i in range(32)])  49 us
    ppermute x36, waiting for transfers between devices, pull(): lax.ppermute(value, 'img', [(i, moved(i, axis, -r)) for i in range(32)])  33.4 us
    unnamed x48, local copies, waits for them, and re-layouts  11.4 us
    ppermute x3, waiting for transfers between devices, pull_z(): return lax.ppermute(value, 'img', [(i, i ^ 16) for i in range(32)])  11.2 us
    ppermute x3, starting transfers between devices, pull_z(): return lax.ppermute(value, 'img', [(i, i ^ 16) for i in range(32)])  10.8 us
  transfers between devices with their start and end apart: 43, of which 15 were waited for; matrix products, arithmetic and copies ran while one was open for 0% of the time, Pallas kernels for 35%

profile of v1, /device:TPU:0, one launch (start us, length us, event | category | flops | bytes accessed | tf_op | source)
XLA Modules:
  0.0 194.5 jit_solution(890511429532189031)
XLA Ops:
  5.9 2.9 %collective-permute-start = (bf16[416,128]{1,0:T(8,128)(2,1)S(1)}, bf16[416,128]{1,0:T(8,128)(2,1)S(1)}, u32[]{:S(2)}, u32[]{:S(2)}) collective-permute-start(bf16[416,128]{1,0:T(8,128)(2,1)S(1)} %get-tuple-element.58), channel_id=1, source_target_pairs={{0,12},{1,13},{2,14},{3,15},{4,0},{5,1},{6,2},{7,3},{8,4},{9,5},{1... | collective-permute-start | bytes 319496 | tf_op jit(solution)/shard_map/ppermute | solution.py:30
  10.5 3.0 %collective-permute-start.3 = (bf16[416,128]{1,0:T(8,128)(2,1)S(1)}, bf16[416,128]{1,0:T(8,128)(2,1)S(1)}, u32[]{:S(2)}, u32[]{:S(2)}) collective-permute-start(bf16[416,128]{1,0:T(8,128)(2,1)S(1)} %get-tuple-element.62), channel_id=1, source_target_pairs={{0,3},{1,0},{2,1},{3,2},{4,7},{5,4},{6,5},{7,6},{8,11},{9,8},{10,9... | collective-permute-start | bytes 319496 | tf_op jit(solution)/shard_map/ppermute | solution.py:30
  15.1 2.2 %copy-done = bf16[256,8192]{1,0:T(8,128)(2,1)S(1)} copy-done((bf16[256,8192]{1,0:T(8,128)(2,1)S(1)}, bf16[256,8192]{1,0:T(8,128)(2,1)}, u32[]{:S(2)}) %copy-start) | copy-done | bytes 4194328
  17.3 2.6 %shard_map.112 = (bf16[256,8192]{1,0:T(8,128)(2,1)S(1)}, f32[256,128]{1,0:T(8,128)S(1)}) custom-call(s32[5]{0:T(128)S(1)} %stack.32.refs_0_, bf16[256,8192]{1,0:T(8,128)(2,1)S(1)} %copy-done, bf16[416,128]{1,0:T(8,128)(2,1)S(1)} %get-tuple-element.56.refs_2_.refs_1_.refs_5_), custom_call_target="tpu_custom_call" | custom-call | flops 2600000000 | bytes 7800000 | tf_op jit(solution)/shard_map/pallas_call | solution.py:54
  25.3 3.9 %collective-permute-start.6 = (bf16[8,144,128]{2,1,0:T(8,128)(2,1)S(1)}, bf16[8,144,128]{2,1,0:T(8,128)(2,1)S(1)}, u32[]{:S(2)}, u32[]{:S(2)}) collective-permute-start(bf16[8,144,128]{2,1,0:T(8,128)(2,1)S(1)} %shard_map.113.refs_3_.refs_1_), channel_id=1, source_target_pairs={{0,16},{1,17},{2,18},{3,19},{4,20},{5,21},{6,22},{7,23},{8,24},{9,... | collective-permute-start | bytes 884744 | tf_op jit(solution)/shard_map/ppermute | solution.py:34
  29.2 5.1 %collective-permute-done.6.refs_2_ = bf16[8,144,128]{2,1,0:T(8,128)(2,1)S(1)} collective-permute-done((bf16[8,144,128]{2,1,0:T(8,128)(2,1)S(1)}, bf16[8,144,128]{2,1,0:T(8,128)(2,1)S(1)}, u32[]{:S(2)}, u32[]{:S(2)}) %collective-permute-start.6) | collective-permute-done | bytes 294944 | tf_op jit(solution)/shard_map/ppermute | solution.py:34
  38.2 2.3 %collective-permute-start.9 = (bf16[8,144,128]{2,1,0:T(8,128)(2,1)S(1)}, bf16[8,144,128]{2,1,0:T(8,128)(2,1)S(1)}, u32[]{:S(2)}, u32[]{:S(2)}) collective-permute-start(bf16[8,144,128]{2,1,0:T(8,128)(2,1)S(1)} %shard_map.115.refs_6_.refs_9_), channel_id=1, source_target_pairs={{0,3},{1,0},{2,1},{3,2},{4,7},{5,4},{6,5},{7,6},{8,11},{9,8},{10,9... | collective-permute-start | bytes 884744 | tf_op jit(solution)/shard_map/ppermute | solution.py:30
  42.6 11.3 %shard_map.117.refs_1_.refs_9_ = f32[256,1024]{1,0:T(8,128)S(1)} custom-call(s32[5]{0:T(128)S(1)} %stack.32.refs_0_, bf16[256,8192]{1,0:T(8,128)(2,1)S(1)} %get-tuple-element.57.refs_1_.refs_2_.refs_3_.refs_5_.refs_6_, bf16[8192,1024]{1,0:T(8,128)(2,1)} %refs_8_.3, bf16[8192,1024]{1,0:T(8,128)(2,1)} %refs_8_.3, bf16[8192,1024]{1,0:T(8,128)(2,1)} %refs_8_.3, ...), custom_call_target="tpu_custom_call" | custom-call | flops 11000000512 | bytes 33000000 | tf_op jit(solution)/shard_map/pallas_call | solution.py:54
  56.5 2.2 %collective-permute-start.14 = (bf16[256,128]{1,0:T(8,128)(2,1)S(1)}, bf16[256,128]{1,0:T(8,128)(2,1)S(1)}, u32[]{:S(2)}, u32[]{:S(2)}) collective-permute-start(bf16[256,128]{1,0:T(8,128)(2,1)S(1)} %get-tuple-element.69), channel_id=1, source_target_pairs={{0,8},{1,9},{2,10},{3,11},{4,12},{5,13},{6,14},{7,15},{8,0},{9,1},... | collective-permute-start | bytes 196616 | tf_op jit(solution)/shard_map/ppermute | solution.py:30
  64.1 2.2 %collective-permute-done.17.refs_7_.refs_3_ = bf16[256,128]{1,0:T(8,128)(2,1)S(1)} collective-permute-done((bf16[256,128]{1,0:T(8,128)(2,1)S(1)}, bf16[256,128]{1,0:T(8,128)(2,1)S(1)}, u32[]{:S(2)}, u32[]{:S(2)}) %collective-permute-start.17) | collective-permute-done | bytes 65568 | tf_op jit(solution)/shard_map/ppermute | solution.py:30
  69.4 2.2 %collective-permute-start.24 = (bf16[8,144,128]{2,1,0:T(8,128)(2,1)S(1)}, bf16[8,144,128]{2,1,0:T(8,128)(2,1)S(1)}, u32[]{:S(2)}, u32[]{:S(2)}) collective-permute-start(bf16[8,144,128]{2,1,0:T(8,128)(2,1)S(1)} %shard_map.120.refs_4_.refs_9_), channel_id=1, source_target_pairs={{0,8},{1,9},{2,10},{3,11},{4,12},{5,13},{6,14},{7,15},{8,0},{9,1},... | collective-permute-start | bytes 884744 | tf_op jit(solution)/shard_map/ppermute | solution.py:30
  71.6 2.2 %collective-permute-start.23 = (bf16[8,144,128]{2,1,0:T(8,128)(2,1)S(1)}, bf16[8,144,128]{2,1,0:T(8,128)(2,1)S(1)}, u32[]{:S(2)}, u32[]{:S(2)}) collective-permute-start(bf16[8,144,128]{2,1,0:T(8,128)(2,1)S(1)} %shard_map.120.refs_4_.refs_9_), channel_id=1, source_target_pairs={{0,12},{1,13},{2,14},{3,15},{4,0},{5,1},{6,2},{7,3},{8,4},{9,5},{1... | collective-permute-start | bytes 884744 | tf_op jit(solution)/shard_map/ppermute | solution.py:30
  75.3 1.9 collective-permute-start.35
  77.3 8.6 %shard_map.122 = (bf16[1296,128]{1,0:T(8,128)(2,1)S(1)}, bf16[1296,128]{1,0:T(8,128)(2,1)S(1)}, bf16[1296,128]{1,0:T(8,128)(2,1)S(1)}, bf16[1296,128]{1,0:T(8,128)(2,1)S(1)}) custom-call(s32[5]{0:T(128)S(1)} %stack.32.refs_0_, bf16[256,128]{1,0:T(8,128)(2,1)S(1)} %get-tuple-element.67.refs_4_.refs_1_, ...), custom_call_target="tpu_custom_call" | custom-call | flops 8499999744 | bytes 25500000 | tf_op jit(solution)/shard_map/pallas_call | solution.py:54
  88.3 8.6 %shard_map.123 = (bf16[1296,128]{1,0:T(8,128)(2,1)S(1)}, bf16[1296,128]{1,0:T(8,128)(2,1)S(1)}, bf16[1296,128]{1,0:T(8,128)(2,1)S(1)}, bf16[1296,128]{1,0:T(8,128)(2,1)S(1)}) custom-call(s32[5]{0:T(128)S(1)} %stack.32.refs_0_, bf16[256,128]{1,0:T(8,128)(2,1)S(1)} %get-tuple-element.81.refs_1_, bf16[256,128]{1,0:T(8,128)(2,1)S(1)} %collective-permute-done.16.refs_6_.refs_2_, ...), custom_call_target="tpu_custom_call" | custom-call | flops 8499999744 | bytes 25500000 | tf_op jit(solution)/shard_map/pallas_call | solution.py:54
  97.6 2.1 %collective-permute-start.26 = (bf16[1296,128]{1,0:T(8,128)(2,1)S(1)}, bf16[1296,128]{1,0:T(8,128)(2,1)S(1)}, u32[]{:S(2)}, u32[]{:S(2)}) collective-permute-start(bf16[1296,128]{1,0:T(8,128)(2,1)S(1)} %get-tuple-element.83), channel_id=1, source_target_pairs={{0,3},{1,0},{2,1},{3,2},{4,7},{5,4},{6,5},{7,6},{8,11},{9,8},{10,9... | collective-permute-start | bytes 995336 | tf_op jit(solution)/shard_map/ppermute | solution.py:30
  103.7 6.8 %shard_map.124 = (bf16[528,512]{1,0:T(8,128)(2,1)}, bf16[528,512]{1,0:T(8,128)(2,1)}, bf16[528,512]{1,0:T(8,128)(2,1)S(1)}, f32[512,512]{1,0:T(8,128)S(1)}, f32[1,512]{1,0:T(1,128)S(1)}) custom-call(s32[5]{0:T(128)S(1)} %stack.32.refs_0_, bf16[1296,128]{1,0:T(8,128)(2,1)S(1)} %get-tuple-element.77.refs_14_.refs_1_, ...), custom_call_target="tpu_custom_call" | custom-call | flops 6000000000 | bytes 18000000 | tf_op jit(solution)/shard_map/pallas_call | solution.py:54
  110.6 2.9 %collective-permute-done.34.refs_2_.refs_8_ = bf16[256,1024]{1,0:T(8,128)(2,1)S(1)} collective-permute-done((bf16[256,1024]{1,0:T(8,128)(2,1)S(1)}, bf16[256,1024]{1,0:T(8,128)(2,1)S(1)}, u32[]{:S(2)}, u32[]{:S(2)}) %collective-permute-start.34) | collective-permute-done | bytes 524320 | tf_op jit(solution)/shard_map/ppermute | solution.py:30
  114.2 4.8 %collective-permute-done.26.refs_6_.refs_2_ = bf16[1296,128]{1,0:T(8,128)(2,1)S(1)} collective-permute-done((bf16[1296,128]{1,0:T(8,128)(2,1)S(1)}, bf16[1296,128]{1,0:T(8,128)(2,1)S(1)}, u32[]{:S(2)}, u32[]{:S(2)}) %collective-permute-start.26) | collective-permute-done | bytes 331808 | tf_op jit(solution)/shard_map/ppermute | solution.py:30
  119.7 3.5 %collective-permute-done.28.refs_8_.refs_4_ = bf16[1296,128]{1,0:T(8,128)(2,1)S(1)} collective-permute-done((bf16[1296,128]{1,0:T(8,128)(2,1)S(1)}, bf16[1296,128]{1,0:T(8,128)(2,1)S(1)}, u32[]{:S(2)}, u32[]{:S(2)}) %collective-permute-start.28) | collective-permute-done | bytes 331808 | tf_op jit(solution)/shard_map/ppermute | solution.py:30
  123.2 8.0 %shard_map.125 = (bf16[256,4096]{1,0:T(8,128)(2,1)}, f32[256,128]{1,0:T(8,128)S(1)}, bf16[256,1024]{1,0:T(8,128)(2,1)S(1)}) custom-call(s32[5]{0:T(128)S(1)} %stack.32.refs_0_, bf16[1296,128]{1,0:T(8,128)(2,1)S(1)} %get-tuple-element.77.refs_14_.refs_1_, bf16[1296,128]{1,0:T(8,128)(2,1)S(1)} %collective-permute-done.20.refs_2_, ...), custom_call_target="tpu_custom_call" | custom-call | flops 8000000000 | bytes 24000000 | tf_op jit(solution)/shard_map/pallas_call | solution.py:54
  131.5 3.2 %collective-permute-start.31 = (bf16[528,512]{1,0:T(8,128)(2,1)}, bf16[528,512]{1,0:T(8,128)(2,1)S(1)}, u32[]{:S(2)}, u32[]{:S(2)}) collective-permute-start(bf16[528,512]{1,0:T(8,128)(2,1)} %get-tuple-element.93), channel_id=1, source_target_pairs={{0,2},{1,3},{2,0},{3,1},{4,6},{5,7},{6,4},{7,5},{8,10},{9,11},{10,... | collective-permute-start | bytes 1622024 | tf_op jit(solution)/shard_map/ppermute | solution.py:30
  137.5 6.6 %shard_map.127 = (bf16[528,512]{1,0:T(8,128)(2,1)}, bf16[528,512]{1,0:T(8,128)(2,1)S(1)}, bf16[528,512]{1,0:T(8,128)(2,1)S(1)}, f32[512,512]{1,0:T(8,128)S(1)}, f32[1,512]{1,0:T(1,128)S(1)}) custom-call(s32[5]{0:T(128)S(1)} %stack.32.refs_0_, bf16[1296,128]{1,0:T(8,128)(2,1)S(1)} %get-tuple-element.82.refs_11_.refs_5_.refs_4_.refs_1_, ...), custom_call_target="tpu_custom_call" | custom-call | flops 6000000000 | bytes 18000000 | tf_op jit(solution)/shard_map/pallas_call | solution.py:54
  146.6 4.1 %shard_map.128.refs_6_ = bf16[256,2048]{1,0:T(8,128)(2,1)S(1)} custom-call(s32[5]{0:T(128)S(1)} %stack.32.refs_0_, bf16[256,1024]{1,0:T(8,128)(2,1)S(1)} %get-tuple-element.88.refs_1_, f32[256,128]{1,0:T(8,128)S(1)} %get-tuple-element.89.refs_2_, f32[256,128]{1,0:T(8,128)S(1)} %get-tuple-element.86.refs_10_.refs_3_, bf16[256,8192]{1,0:T(8,128)(2,1)} %refs_4_.5, ...), custom_call_target="tpu_custom_call" | custom-call | flops 4000000000 | bytes 12000000 | tf_op jit(solution)/shard_map/pallas_call | solution.py:54
  152.0 3.0 %collective-permute-start.40 = (bf16[528,512]{1,0:T(8,128)(2,1)S(1)}, bf16[528,512]{1,0:T(8,128)(2,1)S(1)}, u32[]{:S(2)}, u32[]{:S(2)}) collective-permute-start(bf16[528,512]{1,0:T(8,128)(2,1)S(1)} %copy-done.19), channel_id=1, source_target_pairs={{0,8},{1,9},{2,10},{3,11},{4,12},{5,13},{6,14},{7,15},{8,0},{9,1},... | collective-permute-start | bytes 1622024 | tf_op jit(solution)/shard_map/ppermute | solution.py:30
  155.0 4.2 %collective-permute-done.31.refs_4_ = bf16[528,512]{1,0:T(8,128)(2,1)S(1)} collective-permute-done((bf16[528,512]{1,0:T(8,128)(2,1)}, bf16[528,512]{1,0:T(8,128)(2,1)S(1)}, u32[]{:S(2)}, u32[]{:S(2)}) %collective-permute-start.31) | collective-permute-done | bytes 540704 | tf_op jit(solution)/shard_map/ppermute | solution.py:30
  159.2 3.0 %collective-permute-start.41 = (bf16[528,512]{1,0:T(8,128)(2,1)S(1)}, bf16[528,512]{1,0:T(8,128)(2,1)S(1)}, u32[]{:S(2)}, u32[]{:S(2)}) collective-permute-start(bf16[528,512]{1,0:T(8,128)(2,1)S(1)} %copy-done.17), channel_id=1, source_target_pairs={{0,12},{1,13},{2,14},{3,15},{4,0},{5,1},{6,2},{7,3},{8,4},{9,5},{1... | collective-permute-start | bytes 1622024 | tf_op jit(solution)/shard_map/ppermute | solution.py:30
  163.2 3.3 %collective-permute-start.38 = (bf16[272,512]{1,0:T(8,128)(2,1)S(1)}, bf16[272,512]{1,0:T(8,128)(2,1)S(1)}, u32[]{:S(2)}, u32[]{:S(2)}) collective-permute-start(bf16[272,512]{1,0:T(8,128)(2,1)S(1)} %get-tuple-element.98), channel_id=1, source_target_pairs={{0,16},{1,17},{2,18},{3,19},{4,20},{5,21},{6,22},{7,23},{8,24},{9,... | collective-permute-start | bytes 835592 | tf_op jit(solution)/shard_map/ppermute | solution.py:34
  166.5 4.1 %shard_map.130.refs_9_.refs_1_ = f32[256,2048]{1,0:T(8,128)S(1)} custom-call(s32[5]{0:T(128)S(1)} %stack.32.refs_0_, bf16[256,1024]{1,0:T(8,128)(2,1)S(1)} %get-tuple-element.88.refs_1_, f32[256,128]{1,0:T(8,128)S(1)} %get-tuple-element.89.refs_2_, f32[256,128]{1,0:T(8,128)S(1)} %get-tuple-element.86.refs_10_.refs_3_, bf16[256,8192]{1,0:T(8,128)(2,1)} %refs_4_.5, ...), custom_call_target="tpu_custom_call" | custom-call | flops 4000000000 | bytes 12000000 | tf_op jit(solution)/shard_map/pallas_call | solution.py:54
  172.1 7.1 %collective-permute-done.41.refs_5_ = bf16[528,512]{1,0:T(8,128)(2,1)S(1)} collective-permute-done((bf16[528,512]{1,0:T(8,128)(2,1)S(1)}, bf16[528,512]{1,0:T(8,128)(2,1)S(1)}, u32[]{:S(2)}, u32[]{:S(2)}) %collective-permute-start.41) | collective-permute-done | bytes 540704 | tf_op jit(solution)/shard_map/ppermute | solution.py:30
  181.3 3.7 %collective-permute-start.42 = (bf16[272,512]{1,0:T(8,128)(2,1)S(1)}, bf16[272,512]{1,0:T(8,128)(2,1)S(1)}, u32[]{:S(2)}, u32[]{:S(2)}) collective-permute-start(bf16[272,512]{1,0:T(8,128)(2,1)S(1)} %get-tuple-element.105), channel_id=1, source_target_pairs={{0,16},{1,17},{2,18},{3,19},{4,20},{5,21},{6,22},{7,23},{8,24},{9,... | collective-permute-start | bytes 835592 | tf_op jit(solution)/shard_map/ppermute | solution.py:34
  185.0 6.1 %collective-permute-done.42.refs_7_ = bf16[272,512]{1,0:T(8,128)(2,1)S(1)} collective-permute-done((bf16[272,512]{1,0:T(8,128)(2,1)S(1)}, bf16[272,512]{1,0:T(8,128)(2,1)S(1)}, u32[]{:S(2)}, u32[]{:S(2)}) %collective-permute-start.42) | collective-permute-done | bytes 278560 | tf_op jit(solution)/shard_map/ppermute | solution.py:34
  (134 shorter events, 55.9 us)
Async XLA Ops:
  8.8 11.1 %collective-permute-start.1 = (bf16[416,128]{1,0:T(8,128)(2,1)S(1)}, bf16[416,128]{1,0:T(8,128)(2,1)S(1)}, u32[]{:S(2)}, u32[]{:S(2)}) collective-permute-start(bf16[416,128]{1,0:T(8,128)(2,1)S(1)} %get-tuple-element.59), channel_id=1, source_target_pairs={{0,8},{1,9},{2,10},{3,11},{4,12},{5,13},{6,14},{7,15},{8,0},{9,1},... | collective-permute-start | bytes 319496 | tf_op jit(solution)/shard_map/ppermute | solution.py:30
  9.6 10.3 %collective-permute-start.2 = (bf16[416,128]{1,0:T(8,128)(2,1)S(1)}, bf16[416,128]{1,0:T(8,128)(2,1)S(1)}, u32[]{:S(2)}, u32[]{:S(2)}) collective-permute-start(bf16[416,128]{1,0:T(8,128)(2,1)S(1)} %get-tuple-element.60), channel_id=1, source_target_pairs={{0,4},{1,5},{2,6},{3,7},{4,8},{5,9},{6,10},{7,11},{8,12},{9,13},{1... | collective-permute-start | bytes 319496 | tf_op jit(solution)/shard_map/ppermute | solution.py:30
  22.0 18.5 %collective-permute-start.8 = (bf16[256,1024]{1,0:T(8,128)(2,1)S(1)}, bf16[256,1024]{1,0:T(8,128)(2,1)S(1)}, u32[]{:S(2)}, u32[]{:S(2)}) collective-permute-start(bf16[256,1024]{1,0:T(8,128)(2,1)S(1)} %get-tuple-element.66), channel_id=1, source_target_pairs={{0,4},{1,5},{2,6},{3,7},{4,8},{5,9},{6,10},{7,11},{8,12},{9,13},{1... | collective-permute-start | bytes 1572872 | tf_op jit(solution)/shard_map/ppermute | solution.py:30
  23.9 16.6 %collective-permute-start.7 = (bf16[256,1024]{1,0:T(8,128)(2,1)S(1)}, bf16[256,1024]{1,0:T(8,128)(2,1)S(1)}, u32[]{:S(2)}, u32[]{:S(2)}) collective-permute-start(bf16[256,1024]{1,0:T(8,128)(2,1)S(1)} %get-tuple-element.65.refs_3_), channel_id=1, source_target_pairs={{0,12},{1,13},{2,14},{3,15},{4,0},{5,1},{6,2},{7,3},{8,4},{9,5},{1... | collective-permute-start | bytes 1572872 | tf_op jit(solution)/shard_map/ppermute | solution.py:30
  34.9 19.0 %collective-permute-start.11 = (bf16[8,144,128]{2,1,0:T(8,128)(2,1)S(1)}, bf16[8,144,128]{2,1,0:T(8,128)(2,1)S(1)}, u32[]{:S(2)}, u32[]{:S(2)}) collective-permute-start(bf16[8,144,128]{2,1,0:T(8,128)(2,1)S(1)} %shard_map.115.refs_6_.refs_9_), channel_id=1, source_target_pairs={{0,1},{1,2},{2,3},{3,0},{4,5},{5,6},{6,7},{7,4},{8,9},{9,10},{10,1... | collective-permute-start | bytes 884744 | tf_op jit(solution)/shard_map/ppermute | solution.py:30
  36.5 17.4 %collective-permute-start.10 = (bf16[8,144,128]{2,1,0:T(8,128)(2,1)S(1)}, bf16[8,144,128]{2,1,0:T(8,128)(2,1)S(1)}, u32[]{:S(2)}, u32[]{:S(2)}) collective-permute-start(bf16[8,144,128]{2,1,0:T(8,128)(2,1)S(1)} %shard_map.115.refs_6_.refs_9_), channel_id=1, source_target_pairs={{0,2},{1,3},{2,0},{3,1},{4,6},{5,7},{6,4},{7,5},{8,10},{9,11},{10,... | collective-permute-start | bytes 884744 | tf_op jit(solution)/shard_map/ppermute | solution.py:30
  38.2 15.7 %collective-permute-start.9 = (bf16[8,144,128]{2,1,0:T(8,128)(2,1)S(1)}, bf16[8,144,128]{2,1,0:T(8,128)(2,1)S(1)}, u32[]{:S(2)}, u32[]{:S(2)}) collective-permute-start(bf16[8,144,128]{2,1,0:T(8,128)(2,1)S(1)} %shard_map.115.refs_6_.refs_9_), channel_id=1, source_target_pairs={{0,3},{1,0},{2,1},{3,2},{4,7},{5,4},{6,5},{7,6},{8,11},{9,8},{10,9... | collective-permute-start | bytes 884744 | tf_op jit(solution)/shard_map/ppermute | solution.py:30
  41.1 12.8 %collective-permute-start.12 = (bf16[256,1024]{1,0:T(8,128)(2,1)S(1)}, bf16[256,1024]{1,0:T(8,128)(2,1)S(1)}, u32[]{:S(2)}, u32[]{:S(2)}) collective-permute-start(bf16[256,1024]{1,0:T(8,128)(2,1)S(1)} %shard_map.116.refs_7_), channel_id=1, source_target_pairs={{0,8},{1,9},{2,10},{3,11},{4,12},{5,13},{6,14},{7,15},{8,0},{9,1},... | collective-permute-start | bytes 1572872 | tf_op jit(solution)/shard_map/ppermute | solution.py:30
  55.3 12.7 %collective-permute-start.19 = (bf16[3,256,1024]{2,1,0:T(8,128)(2,1)S(1)}, bf16[3,256,1024]{2,1,0:T(8,128)(2,1)S(1)}, u32[]{:S(2)}, u32[]{:S(2)}) collective-permute-start(bf16[3,256,1024]{2,1,0:T(8,128)(2,1)S(1)} %shard_map.119), channel_id=1, source_target_pairs={{0,32},{32,0},{64,96},{96,64},{1,33},{33,1},{65,97},{97,65},{2,34}... | collective-permute-start | bytes 4718600 | tf_op jit(solution)/shard_map/ppermute | solution.py:38
  68.5 17.4 %collective-permute-start.25 = (bf16[8,144,128]{2,1,0:T(8,128)(2,1)S(1)}, bf16[8,144,128]{2,1,0:T(8,128)(2,1)S(1)}, u32[]{:S(2)}, u32[]{:S(2)}) collective-permute-start(bf16[8,144,128]{2,1,0:T(8,128)(2,1)S(1)} %shard_map.120.refs_4_.refs_9_), channel_id=1, source_target_pairs={{0,4},{1,5},{2,6},{3,7},{4,8},{5,9},{6,10},{7,11},{8,12},{9,13},{1... | collective-permute-start | bytes 884744 | tf_op jit(solution)/shard_map/ppermute | solution.py:30
  69.4 16.6 %collective-permute-start.24 = (bf16[8,144,128]{2,1,0:T(8,128)(2,1)S(1)}, bf16[8,144,128]{2,1,0:T(8,128)(2,1)S(1)}, u32[]{:S(2)}, u32[]{:S(2)}) collective-permute-start(bf16[8,144,128]{2,1,0:T(8,128)(2,1)S(1)} %shard_map.120.refs_4_.refs_9_), channel_id=1, source_target_pairs={{0,8},{1,9},{2,10},{3,11},{4,12},{5,13},{6,14},{7,15},{8,0},{9,1},... | collective-permute-start | bytes 884744 | tf_op jit(solution)/shard_map/ppermute | solution.py:30
  71.6 16.3 %collective-permute-start.23 = (bf16[8,144,128]{2,1,0:T(8,128)(2,1)S(1)}, bf16[8,144,128]{2,1,0:T(8,128)(2,1)S(1)}, u32[]{:S(2)}, u32[]{:S(2)}) collective-permute-start(bf16[8,144,128]{2,1,0:T(8,128)(2,1)S(1)} %shard_map.120.refs_4_.refs_9_), channel_id=1, source_target_pairs={{0,12},{1,13},{2,14},{3,15},{4,0},{5,1},{6,2},{7,3},{8,4},{9,5},{1... | collective-permute-start | bytes 884744 | tf_op jit(solution)/shard_map/ppermute | solution.py:30
  75.2 26.9 %collective-permute-start.33 = (bf16[256,1024]{1,0:T(8,128)(2,1)S(1)}, bf16[256,1024]{1,0:T(8,128)(2,1)S(1)}, u32[]{:S(2)}, u32[]{:S(2)}) collective-permute-start(bf16[256,1024]{1,0:T(8,128)(2,1)S(1)} %get-tuple-element.74.refs_14_), channel_id=1, source_target_pairs={{0,3},{1,0},{2,1},{3,2},{4,7},{5,4},{6,5},{7,6},{8,11},{9,8},{10,9... | collective-permute-start | bytes 1572872 | tf_op jit(solution)/shard_map/ppermute | solution.py:30
  75.3 35.2 %collective-permute-start.35 = (bf16[256,1024]{1,0:T(8,128)(2,1)S(1)}, bf16[256,1024]{1,0:T(8,128)(2,1)S(1)}, u32[]{:S(2)}, u32[]{:S(2)}) collective-permute-start(bf16[256,1024]{1,0:T(8,128)(2,1)S(1)} %get-tuple-element.75.refs_15_), channel_id=1, source_target_pairs={{0,1},{1,2},{2,3},{3,0},{4,5},{5,6},{6,7},{7,4},{8,9},{9,10},{10,1... | collective-permute-start | bytes 1572872 | tf_op jit(solution)/shard_map/ppermute | solution.py:30
  85.9 11.1 %collective-permute-start.20 = (bf16[1296,128]{1,0:T(8,128)(2,1)S(1)}, bf16[1296,128]{1,0:T(8,128)(2,1)S(1)}, u32[]{:S(2)}, u32[]{:S(2)}) collective-permute-start(bf16[1296,128]{1,0:T(8,128)(2,1)S(1)} %get-tuple-element.78), channel_id=1, source_target_pairs={{0,12},{1,13},{2,14},{3,15},{4,0},{5,1},{6,2},{7,3},{8,4},{9,5},{1... | collective-permute-start | bytes 995336 | tf_op jit(solution)/shard_map/ppermute | solution.py:30
  86.0 11.7 %collective-permute-start.21 = (bf16[1296,128]{1,0:T(8,128)(2,1)S(1)}, bf16[1296,128]{1,0:T(8,128)(2,1)S(1)}, u32[]{:S(2)}, u32[]{:S(2)}) collective-permute-start(bf16[1296,128]{1,0:T(8,128)(2,1)S(1)} %get-tuple-element.79), channel_id=1, source_target_pairs={{0,8},{1,9},{2,10},{3,11},{4,12},{5,13},{6,14},{7,15},{8,0},{9,1},... | collective-permute-start | bytes 995336 | tf_op jit(solution)/shard_map/ppermute | solution.py:30
  87.8 13.0 %collective-permute-start.22 = (bf16[1296,128]{1,0:T(8,128)(2,1)S(1)}, bf16[1296,128]{1,0:T(8,128)(2,1)S(1)}, u32[]{:S(2)}, u32[]{:S(2)}) collective-permute-start(bf16[1296,128]{1,0:T(8,128)(2,1)S(1)} %get-tuple-element.80), channel_id=1, source_target_pairs={{0,4},{1,5},{2,6},{3,7},{4,8},{5,9},{6,10},{7,11},{8,12},{9,13},{1... | collective-permute-start | bytes 995336 | tf_op jit(solution)/shard_map/ppermute | solution.py:30
  96.9 16.5 %collective-permute-start.34 = (bf16[256,1024]{1,0:T(8,128)(2,1)S(1)}, bf16[256,1024]{1,0:T(8,128)(2,1)S(1)}, u32[]{:S(2)}, u32[]{:S(2)}) collective-permute-start(bf16[256,1024]{1,0:T(8,128)(2,1)S(1)} %get-tuple-element.76.refs_16_), channel_id=1, source_target_pairs={{0,2},{1,3},{2,0},{3,1},{4,6},{5,7},{6,4},{7,5},{8,10},{9,11},{10,... | collective-permute-start | bytes 1572872 | tf_op jit(solution)/shard_map/ppermute | solution.py:30
  97.6 21.3 %collective-permute-start.26 = (bf16[1296,128]{1,0:T(8,128)(2,1)S(1)}, bf16[1296,128]{1,0:T(8,128)(2,1)S(1)}, u32[]{:S(2)}, u32[]{:S(2)}) collective-permute-start(bf16[1296,128]{1,0:T(8,128)(2,1)S(1)} %get-tuple-element.83), channel_id=1, source_target_pairs={{0,3},{1,0},{2,1},{3,2},{4,7},{5,4},{6,5},{7,6},{8,11},{9,8},{10,9... | collective-permute-start | bytes 995336 | tf_op jit(solution)/shard_map/ppermute | solution.py:30
  100.8 18.8 %collective-permute-start.27 = (bf16[1296,128]{1,0:T(8,128)(2,1)S(1)}, bf16[1296,128]{1,0:T(8,128)(2,1)S(1)}, u32[]{:S(2)}, u32[]{:S(2)}) collective-permute-start(bf16[1296,128]{1,0:T(8,128)(2,1)S(1)} %get-tuple-element.84), channel_id=1, source_target_pairs={{0,2},{1,3},{2,0},{3,1},{4,6},{5,7},{6,4},{7,5},{8,10},{9,11},{10,... | collective-permute-start | bytes 995336 | tf_op jit(solution)/shard_map/ppermute | solution.py:30
  102.1 21.1 %collective-permute-start.28 = (bf16[1296,128]{1,0:T(8,128)(2,1)S(1)}, bf16[1296,128]{1,0:T(8,128)(2,1)S(1)}, u32[]{:S(2)}, u32[]{:S(2)}) collective-permute-start(bf16[1296,128]{1,0:T(8,128)(2,1)S(1)} %get-tuple-element.85), channel_id=1, source_target_pairs={{0,1},{1,2},{2,3},{3,0},{4,5},{5,6},{6,7},{7,4},{8,9},{9,10},{10,1... | collective-permute-start | bytes 995336 | tf_op jit(solution)/shard_map/ppermute | solution.py:30
  114.1 20.7 %collective-permute-start.36 = (bf16[3,256,1024]{2,1,0:T(8,128)(2,1)S(1)}, bf16[3,256,1024]{2,1,0:T(8,128)(2,1)S(1)}, u32[]{:S(2)}, u32[]{:S(2)}) collective-permute-start(bf16[3,256,1024]{2,1,0:T(8,128)(2,1)S(1)} %shard_map.126), channel_id=1, source_target_pairs={{0,32},{32,0},{64,96},{96,64},{1,33},{33,1},{65,97},{97,65},{2,34}... | collective-permute-start | bytes 4718600 | tf_op jit(solution)/shard_map/ppermute | solution.py:38
  131.2 15.4 %collective-permute-start.29 = (bf16[256,4096]{1,0:T(8,128)(2,1)}, bf16[256,4096]{1,0:T(8,128)(2,1)S(1)}, u32[]{:S(2)}, u32[]{:S(2)}) collective-permute-start(bf16[256,4096]{1,0:T(8,128)(2,1)} %get-tuple-element.90.refs_11_), channel_id=1, source_target_pairs={{0,32},{32,0},{64,96},{96,64},{1,33},{33,1},{65,97},{97,65},{2,34}... | collective-permute-start | bytes 6291464 | tf_op jit(solution)/shard_map/ppermute | solution.py:38
  131.2 30.9 %collective-permute-start.30 = (bf16[528,512]{1,0:T(8,128)(2,1)}, bf16[528,512]{1,0:T(8,128)(2,1)S(1)}, u32[]{:S(2)}, u32[]{:S(2)}) collective-permute-start(bf16[528,512]{1,0:T(8,128)(2,1)} %get-tuple-element.87.refs_16_), channel_id=1, source_target_pairs={{0,1},{1,2},{2,3},{3,0},{4,5},{5,6},{6,7},{7,4},{8,9},{9,10},{10,1... | collective-permute-start | bytes 1622024 | tf_op jit(solution)/shard_map/ppermute | solution.py:30
  131.5 27.6 %collective-permute-start.31 = (bf16[528,512]{1,0:T(8,128)(2,1)}, bf16[528,512]{1,0:T(8,128)(2,1)S(1)}, u32[]{:S(2)}, u32[]{:S(2)}) collective-permute-start(bf16[528,512]{1,0:T(8,128)(2,1)} %get-tuple-element.93), channel_id=1, source_target_pairs={{0,2},{1,3},{2,0},{3,1},{4,6},{5,7},{6,4},{7,5},{8,10},{9,11},{10,... | collective-permute-start | bytes 1622024 | tf_op jit(solution)/shard_map/ppermute | solution.py:30
  134.8 27.4 %collective-permute-start.32 = (bf16[528,512]{1,0:T(8,128)(2,1)}, bf16[528,512]{1,0:T(8,128)(2,1)S(1)}, u32[]{:S(2)}, u32[]{:S(2)}) collective-permute-start(bf16[528,512]{1,0:T(8,128)(2,1)} %copy-done.15), channel_id=1, source_target_pairs={{0,3},{1,0},{2,1},{3,2},{4,7},{5,4},{6,5},{7,6},{8,11},{9,8},{10,9... | collective-permute-start | bytes 1622024 | tf_op jit(solution)/shard_map/ppermute | solution.py:30
  150.7 42.0 %collective-permute-start.37 = (bf16[256,2048]{1,0:T(8,128)(2,1)S(1)}, bf16[256,2048]{1,0:T(8,128)(2,1)S(1)}, u32[]{:S(2)}, u32[]{:S(2)}) collective-permute-start(bf16[256,2048]{1,0:T(8,128)(2,1)S(1)} %shard_map.128.refs_6_), channel_id=1, source_target_pairs={{0,64},{32,96},{64,0},{96,32},{1,65},{33,97},{65,1},{97,33},{2,66}... | collective-permute-start | bytes 3145736 | tf_op jit(solution)/shard_map/ppermute | solution.py:38
  152.0 20.1 %collective-permute-start.40 = (bf16[528,512]{1,0:T(8,128)(2,1)S(1)}, bf16[528,512]{1,0:T(8,128)(2,1)S(1)}, u32[]{:S(2)}, u32[]{:S(2)}) collective-permute-start(bf16[528,512]{1,0:T(8,128)(2,1)S(1)} %copy-done.19), channel_id=1, source_target_pairs={{0,8},{1,9},{2,10},{3,11},{4,12},{5,13},{6,14},{7,15},{8,0},{9,1},... | collective-permute-start | bytes 1622024 | tf_op jit(solution)/shard_map/ppermute | solution.py:30
  159.2 20.0 %collective-permute-start.41 = (bf16[528,512]{1,0:T(8,128)(2,1)S(1)}, bf16[528,512]{1,0:T(8,128)(2,1)S(1)}, u32[]{:S(2)}, u32[]{:S(2)}) collective-permute-start(bf16[528,512]{1,0:T(8,128)(2,1)S(1)} %copy-done.17), channel_id=1, source_target_pairs={{0,12},{1,13},{2,14},{3,15},{4,0},{5,1},{6,2},{7,3},{8,4},{9,5},{1... | collective-permute-start | bytes 1622024 | tf_op jit(solution)/shard_map/ppermute | solution.py:30
  162.1 17.1 %collective-permute-start.39 = (bf16[528,512]{1,0:T(8,128)(2,1)}, bf16[528,512]{1,0:T(8,128)(2,1)S(1)}, u32[]{:S(2)}, u32[]{:S(2)}) collective-permute-start(bf16[528,512]{1,0:T(8,128)(2,1)} %get-tuple-element.95.refs_10_), channel_id=1, source_target_pairs={{0,4},{1,5},{2,6},{3,7},{4,8},{5,9},{6,10},{7,11},{8,12},{9,13},{1... | collective-permute-start | bytes 1622024 | tf_op jit(solution)/shard_map/ppermute | solution.py:30
  163.2 21.8 %collective-permute-start.38 = (bf16[272,512]{1,0:T(8,128)(2,1)S(1)}, bf16[272,512]{1,0:T(8,128)(2,1)S(1)}, u32[]{:S(2)}, u32[]{:S(2)}) collective-permute-start(bf16[272,512]{1,0:T(8,128)(2,1)S(1)} %get-tuple-element.98), channel_id=1, source_target_pairs={{0,16},{1,17},{2,18},{3,19},{4,20},{5,21},{6,22},{7,23},{8,24},{9,... | collective-permute-start | bytes 835592 | tf_op jit(solution)/shard_map/ppermute | solution.py:34
  181.3 9.8 %collective-permute-start.42 = (bf16[272,512]{1,0:T(8,128)(2,1)S(1)}, bf16[272,512]{1,0:T(8,128)(2,1)S(1)}, u32[]{:S(2)}, u32[]{:S(2)}) collective-permute-start(bf16[272,512]{1,0:T(8,128)(2,1)S(1)} %get-tuple-element.105), channel_id=1, source_target_pairs={{0,16},{1,17},{2,18},{3,19},{4,20},{5,21},{6,22},{7,23},{8,24},{9,... | collective-permute-start | bytes 835592 | tf_op jit(solution)/shard_map/ppermute | solution.py:34
  (35 other events, 241.0 us)

commit v2 on v1

--- a/solution.py
+++ b/solution.py
@@ -129,20 +129,24 @@
     normed_ref[...] = (x * inverse).astype(BF16)
 
 
-def query_body(pos, normed_ref, w0, w1, w2, w3, query_ref):
-    step = pl.program_id(0)
-    part = None
-    for n, w_ref in enumerate((w0, w1, w2, w3)):
-        term = jnp.dot(normed_ref[:, n * 256:(n + 1) * 256], w_ref[...], preferred_element_type=F32)
-        part = term if part is None else part + term
-
-    @pl.when(step == 0)
-    def _():
-        query_ref[...] = part
-
-    @pl.when(step != 0)
-    def _():
-        query_ref[...] += part
+def fetch(pairs, sem):
+    copies = [pltpu.make_async_copy(source, target, sem.at[n]) for n, (source, target) in enumerate(pairs)]
+    for copy in copies:
+        copy.start()
+    return copies
+
+
+def query_body(pos, normed_ref, w_ref, query_ref, normed_buf, w_buf, sem):
+    pairs = []
+    for i in range(8):
+        pairs.append((normed_ref.at[:, i * 1024:(i + 1) * 1024], normed_buf.at[i]))
+        pairs.append((w_ref.at[i * 1024:(i + 1) * 1024], w_buf.at[i]))
+    copies = fetch(pairs, sem)
+    for i in range(8):
+        copies[2 * i].wait()
+        copies[2 * i + 1].wait()
+        part = jnp.dot(normed_buf[i], w_buf[i], preferred_element_type=F32)
+        query_ref[...] = part if i == 0 else query_ref[...] + part
 
 
 def chunks_body(pos, query_ref, *outs):
@@ -296,35 +300,43 @@
         grad_ref[:, columns] = (sum_ref[...] + sum_parts(got_ref[256:272])) * (1.0 - t * t)
 
 
-def partial_grad(grad, w_refs):
-    dims = (((1,), (1,)), ((), ()))
-    return jnp.concatenate(
-        [lax.dot_general(grad, w_ref[...], dims, preferred_element_type=F32) for w_ref in w_refs], 1
+def weight_rows(w_ref, w_buf, sem, blocks):
+    return fetch(
+        [(w_ref.at[pl.ds(pl.multiple_of(block * 1024, 1024), 1024)], w_buf.at[n]) for n, block in enumerate(blocks)], sem
     )
+
+
+def partial_grad(grad, w, x, inverse, share):
+    part = lax.dot_general(grad, w, (((1,), (1,)), ((), ())), preferred_element_type=F32)
+    return part - x.astype(F32) * inverse * share
 
 
 def input_first_body(pos, *refs):
     messages = refs[0:8]
-    query_ref, inverse_ref, x_ref, w0, w1, w2, w3, send_ref, share_ref, grad_ref = refs[8:]
-
-    @pl.when(pl.program_id(0) == 0)
-    def _():
-        for s in range(2):
-            for r in range(4):
-                column = s * 512 + ((pos[X + s] + r) % 4) * 128
-                source = ((4 - r) % 4) * 256
-                grad_ref[:, lanes(column, 128)] = messages[s * 4 + r][source:source + 256]
-        share = jnp.sum(grad_ref[...].astype(F32) * query_ref[...], axis=1, keepdims=True)
-        share_ref[...] = jnp.broadcast_to(share * (1.0 / 8192.0), share_ref.shape)
-
-    h = x_ref[...].astype(F32) * inverse_ref[:, :1]
-    send_ref[...] = (partial_grad(grad_ref[...], (w0, w1, w2, w3)) - h * share_ref[:, :1]).astype(BF16)
-
-
-def input_next_body(pos, grad_ref, share_ref, inverse_ref, x_ref, w0, w1, w2, w3, got_ref, out_ref):
-    h = x_ref[...].astype(F32) * inverse_ref[:, :1]
-    out = partial_grad(grad_ref[...], (w0, w1, w2, w3)) - h * share_ref[:, :1] + got_ref[...].astype(F32)
-    out_ref[...] = out.astype(out_ref.dtype)
+    query_ref, inverse_ref, x0, x1, w_ref, send_ref, share_ref, grad_ref, w_buf, sem = refs[8:]
+    copies = weight_rows(w_ref, w_buf, sem, [(i // 2) * 4 + (1 - pos[CORE]) * 2 + i % 2 for i in range(4)])
+    for s in range(2):
+        for r in range(4):
+            column = s * 512 + ((pos[X + s] + r) % 4) * 128
+            source = ((4 - r) % 4) * 256
+            grad_ref[:, lanes(column, 128)] = messages[s * 4 + r][source:source + 256]
+    grad = grad_ref[...]
+    share = jnp.sum(grad.astype(F32) * query_ref[...], axis=1, keepdims=True) * (1.0 / 8192.0)
+    share_ref[...] = jnp.broadcast_to(share, share_ref.shape)
+    for i in range(4):
+        x = (x0, x1)[i // 2][:, (i % 2) * 1024:(i % 2 + 1) * 1024]
+        copies[i].wait()
+        out = partial_grad(grad, w_buf[i], x, inverse_ref[:, :1], share)
+        send_ref[:, i * 1024:(i + 1) * 1024] = out.astype(BF16)
+
+
+def input_next_body(z_of, pos, grad_ref, share_ref, inverse_ref, x_ref, got_ref, w_ref, out_ref, w_buf, sem):
+    copies = weight_rows(w_ref, w_buf, sem, [z_of(pos) * 4 + pos[CORE] * 2 + i for i in range(2)])
+    for i in range(2):
+        columns = slice(i * 1024, (i + 1) * 1024)
+        copies[i].wait()
+        out = partial_grad(grad_ref[...], w_buf[i], x_ref[:, columns], inverse_ref[:, :1], share_ref[:, :1])
+        out_ref[:, columns] = (out + got_ref[:, columns].astype(F32)).astype(out_ref.dtype)
 
 
 def input_last_body(pos, keep_ref, got_ref, inverse_ref, out_ref):
@@ -405,16 +417,20 @@
 
     early = cut(0, (1, 3), [near])
     got_x = [pull(early[0], "x", 1), None, pull(early[1], "x", 3)]
+    early = cut(1, (1, 3), early)
+    got_y = [pull(early[0], "y", 1), None, pull(early[1], "y", 3)]
     quarters = [merge(0, [], [early[0]])[0]]
-    early = cut(0, (2,), [got_x[0], got_x[2]])
+    early = cut(0, (2,), [got_x[0], got_x[2], got_y[0], got_y[2]])
     got_x[1] = pull(early[0], "x", 2)
+    anywhere = pl.BlockSpec(memory_space=pl.ANY)
     query = call(
-        query_body, pos, [normed] + [w_query] * 4,
-        [like((256, 1024), F32)],
-        in_specs=[
-            pl.BlockSpec((256, 1024), lambda i, pos: (0, i)),
-        ] + [pl.BlockSpec((256, 1024), lambda i, pos, n=n: (i * 4 + n, 0)) for n in range(4)],
-        grid=(8,), after=[quarters[0][0], early[0]], us=11.0, vmem=48,
+        query_body, pos, [normed, w_query], [like((256, 1024), F32)], in_specs=[anywhere] * 2,
+        scratch=[
+            pltpu.VMEM((8, 256, 1024), BF16),
+            pltpu.VMEM((8, 1024, 1024), BF16),
+            pltpu.SemaphoreType.DMA((16,)),
+        ],
+        after=[quarters[0][0], early[0]], us=11.0, vmem=44,
     )[0]
     chunks = call(chunks_body, pos, [query], [like((256, 128))] * 8, after=quarters[0][1:] + [got_x[1]])
     swapped = [pull_text(stack(got_x, [chunks[0]]), 1)]
@@ -422,10 +438,10 @@
         [chunks[s * 4]] + [pull(chunks[s * 4 + r], axis, r) for r in (1, 2, 3)] for s, (axis, other) in enumerate(AXES)
     ]
     quarters.append(merge(1, [], queries[0][1:] + queries[1][1:] + swapped)[0])
-    late = cut(1, (1, 3, 2), [quarters[1][0]])
+    late = cut(1, (2,), [quarters[1][0]])
     results = [attend(0, late)]
     results.append(attend(1, [results[0][0]]))
-    got_y = [pull(late[(0, 2, 1)[r - 1]], "y", r) for r in (1, 2, 3)]
+    got_y[1] = pull(late[0], "y", 2)
     swapped.append(pull_text(stack(got_y, [results[1][0]]), 1))
     parts = [[normed, normed] + got + [swapped[s]] for s, got in enumerate((got_x, got_y))]
 
@@ -453,7 +469,7 @@
             [like((528, 512))] * 3 + [like((512, 512), F32), like((1, 512), F32)],
             in_specs=[None] * 4 + part_specs(s, lambda i: i + 1),
             scratch=[pltpu.VMEM((1024, 512), BF16)],
-            grid=(4,), after=after, us=6.0,
+            grid=(4,), after=after, us=6.0 if s == 0 else 0.1,
         )
         got = [pull(v, AXES[s][1], -m) for v, m in zip(sends, (1, 2, 3))]
         return [keep, gate_sum] + got, sends[0]
@@ -461,34 +477,29 @@
     def third(s, values, after):
         message, keep, gate_total = call(
             third_body, pos, values, [like((272, 512)), like((256, 512), F32), like((1, 512), F32)],
-            scratch=[pltpu.VMEM((2, 256, 512), F32)], after=after,
+            scratch=[pltpu.VMEM((2, 256, 512), F32)], after=after, us=0.1,
         )
         return [keep, gate_total, pull_z(message)]
 
-    def column_specs(block):
-        return [
-            pl.BlockSpec((256, 1024), lambda i, pos: (0, block(i, pos))),
-        ] + [pl.BlockSpec((256, 1024), lambda i, pos, n=n: (block(i, pos) * 4 + n, 0)) for n in range(4)]
-
     values0, done0 = first_chunks(0, [results[1][0]])
+    columns = lambda block: pl.BlockSpec((256, 2048), lambda i, pos: (0, block(pos)))
     send, share, grad_own = call(
-        input_first_body, pos, messages[0] + messages[1] + [query, inverse, text_in] + [w_query] * 4,
+        input_first_body, pos, messages[0] + messages[1] + [query, inverse, text_in, text_in, w_query],
         [like((256, 4096)), like((256, 128), F32), like((256, 1024))],
-        in_specs=[None] * 10 + column_specs(lambda i, pos: (i // 2) * 4 + (1 - pos[CORE]) * 2 + i % 2),
-        out_specs=[pl.BlockSpec((256, 1024), lambda i, pos: (0, i)), None, None],
-        grid=(4,), after=[done0], us=8.0, vmem=48,
+        in_specs=[None] * 10
+        + [columns(lambda pos: 1 - pos[CORE]), columns(lambda pos: 3 - pos[CORE]), anywhere],
+        scratch=[pltpu.VMEM((4, 1024, 1024), BF16), pltpu.SemaphoreType.DMA((4,))],
+        after=[done0], us=8.0, vmem=40,
     )
     got_core = pull_text(send, 1)
 
     def input_next(z_of, dtype, after):
         return call(
-            input_next_body, pos, [grad_own, share, inverse, text_in] + [w_query] * 4 + [got_core],
+            functools.partial(input_next_body, z_of), pos, [grad_own, share, inverse, text_in, got_core, w_query],
             [like((256, 2048), dtype)],
-            in_specs=[None] * 3
-            + column_specs(lambda i, pos: z_of(pos) * 4 + pos[CORE] * 2 + i)
-            + [pl.BlockSpec((256, 1024), lambda i, pos: (0, z_of(pos) * 2 + i))],
-            out_specs=[pl.BlockSpec((256, 1024), lambda i, pos: (0, i))],
-            grid=(2,), after=after, us=4.0, vmem=48,
+            in_specs=[None] * 3 + [columns(lambda pos: z_of(pos) * 2 + pos[CORE]), columns(z_of), anywhere],
+            scratch=[pltpu.VMEM((2, 1024, 1024), BF16), pltpu.SemaphoreType.DMA((2,))],
+            after=after, us=0.1, vmem=40,
         )[0]
 
     values1, done1 = first_chunks(1, [send])
@@ -496,12 +507,12 @@
     closing = third(0, values0, [send_z_lo])
     got_z_lo = pull_text(send_z_lo, 2)
     keep_input = input_next(lambda pos: pos[Z_LO], F32, [closing[0]])
-    attended = call(home_body, pos, messages[0] + messages[1], [like((256, 1024))], after=[keep_input])[0]
+    attended = call(home_body, pos, messages[0] + messages[1], [like((256, 1024))], after=[keep_input], us=0.1)[0]
     closing += third(1, values1, [attended])
+    input_grad = call(input_last_body, pos, [keep_input, got_z_lo, inverse], [like((256, 2048))])[0]
     query_weight_grad, gate_grad = call(
-        last_body, pos, [gate_row] + closing, [like((256, 1024), F32), like((1, 1024), F32)], after=[closing[3]]
+        last_body, pos, [gate_row] + closing, [like((256, 1024), F32), like((1, 1024), F32)], after=[closing[3], input_grad]
     )
-    input_grad = call(input_last_body, pos, [keep_input, got_z_lo, inverse], [like((256, 2048))])[0]
     return (attended, input_grad, query_weight_grad, gate_grad.reshape(1024))
 
 

time: 196 us -> 185 us (0.944)
  Pallas kernels: 74.6 us -> 67.2 us
  local copies, waits for them, and re-layouts: 11.5 us -> 9.13 us
    pallas_call x24 -> x25, Pallas kernels: 74.6 us -> 67.2 us  [call(): pl.pallas_call(kernel, grid_spec=pltpu.PrefetchScalarGridSpec(num_scalar_...]
    ppermute x36, starting transfers between devices: 49 us -> 46.2 us  [pull(): lax.ppermute(value, 'img', [(i, moved(i, axis, -r)) for i in range(32)])]
    unnamed x48 -> x32, local copies, waits for them, and re-layouts: 11.4 us -> 8.96 us
    ppermute x4, waiting for transfers between devices: 0.01 us -> 2.29 us  [pull_text(): return lax.ppermute(value, 'text', [(i, i ^ bit) for i in range(4)])]
  transfers between devices with their start and end apart: 43 -> 43, of which waited for: 15 -> 17; matrix products, arithmetic and copies ran while one was open for 0% -> 0% of each run, Pallas kernels for 35% -> 33%
where the time goes in v2:
time: 185 us; the launch traced here: 184 us
  Pallas kernels  67.2 us (36%)
  starting transfers between devices  60.4 us (33%)
  waiting for transfers between devices  45.3 us (24%)
  local copies, waits for them, and re-layouts  9.13 us (5%)
    pallas_call x25, Pallas kernels, call(): pl.pallas_call(kernel, grid_spec=pltpu.PrefetchScalarGridSpec(num_scalar_...  67.2 us
    ppermute x36, starting transfers between devices, pull(): lax.ppermute(value, 'img', [(i, moved(i, axis, -r)) for i in range(32)])  46.2 us
    ppermute x36, waiting for transfers between devices, pull(): lax.ppermute(value, 'img', [(i, moved(i, axis, -r)) for i in range(32)])  33.2 us
    ppermute x3, starting transfers between devices, pull_z(): return lax.ppermute(value, 'img', [(i, i ^ 16) for i in range(32)])  11.1 us
    ppermute x3, waiting for transfers between devices, pull_z(): return lax.ppermute(value, 'img', [(i, i ^ 16) for i in range(32)])  9.8 us
    unnamed x32, local copies, waits for them, and re-layouts  8.96 us
  transfers between devices with their start and end apart: 43, of which 17 were waited for; matrix products, arithmetic and copies ran while one was open for 0% of the time, Pallas kernels for 33%

profile of v2, /device:TPU:0, one launch (start us, length us, event | category | flops | bytes accessed | tf_op | source)
XLA Modules:
  0.0 184.3 jit_solution(9942147820167223574)
XLA Ops:
  5.9 2.9 %collective-permute-start = (bf16[416,128]{1,0:T(8,128)(2,1)S(1)}, bf16[416,128]{1,0:T(8,128)(2,1)S(1)}, u32[]{:S(2)}, u32[]{:S(2)}) collective-permute-start(bf16[416,128]{1,0:T(8,128)(2,1)S(1)} %get-tuple-element.57), channel_id=1, source_target_pairs={{0,12},{1,13},{2,14},{3,15},{4,0},{5,1},{6,2},{7,3},{8,4},{9,5},{1... | collective-permute-start | bytes 319496 | tf_op jit(solution)/shard_map/ppermute | solution.py:30
  10.5 3.0 %collective-permute-start.3 = (bf16[416,128]{1,0:T(8,128)(2,1)S(1)}, bf16[416,128]{1,0:T(8,128)(2,1)S(1)}, u32[]{:S(2)}, u32[]{:S(2)}) collective-permute-start(bf16[416,128]{1,0:T(8,128)(2,1)S(1)} %get-tuple-element.61), channel_id=1, source_target_pairs={{0,3},{1,0},{2,1},{3,2},{4,7},{5,4},{6,5},{7,6},{8,11},{9,8},{10,9... | collective-permute-start | bytes 319496 | tf_op jit(solution)/shard_map/ppermute | solution.py:30
  15.1 2.2 %copy-done = bf16[256,8192]{1,0:T(8,128)(2,1)S(1)} copy-done((bf16[256,8192]{1,0:T(8,128)(2,1)S(1)}, bf16[256,8192]{1,0:T(8,128)(2,1)}, u32[]{:S(2)}) %copy-start) | copy-done | bytes 4194328
  17.3 2.6 %shard_map.112 = (bf16[256,8192]{1,0:T(8,128)(2,1)S(1)}, f32[256,128]{1,0:T(8,128)S(1)}) custom-call(s32[5]{0:T(128)S(1)} %stack.32.refs_0_, bf16[256,8192]{1,0:T(8,128)(2,1)S(1)} %copy-done, bf16[416,128]{1,0:T(8,128)(2,1)S(1)} %get-tuple-element.55.refs_2_.refs_1_.refs_5_), custom_call_target="tpu_custom_call" | custom-call | flops 2600000000 | bytes 7800000 | tf_op jit(solution)/shard_map/pallas_call | solution.py:54
  22.0 2.7 %collective-permute-start.7 = (bf16[256,1024]{1,0:T(8,128)(2,1)S(1)}, bf16[256,1024]{1,0:T(8,128)(2,1)S(1)}, u32[]{:S(2)}, u32[]{:S(2)}) collective-permute-start(bf16[256,1024]{1,0:T(8,128)(2,1)S(1)} %get-tuple-element.64.refs_3_), channel_id=1, source_target_pairs={{0,12},{1,13},{2,14},{3,15},{4,0},{5,1},{6,2},{7,3},{8,4},{9,5},{1... | collective-permute-start | bytes 1572872 | tf_op jit(solution)/shard_map/ppermute | solution.py:30
  29.2 3.9 %collective-permute-start.6 = (bf16[8,144,128]{2,1,0:T(8,128)(2,1)S(1)}, bf16[8,144,128]{2,1,0:T(8,128)(2,1)S(1)}, u32[]{:S(2)}, u32[]{:S(2)}) collective-permute-start(bf16[8,144,128]{2,1,0:T(8,128)(2,1)S(1)} %shard_map.113.refs_3_.refs_1_), channel_id=1, source_target_pairs={{0,16},{1,17},{2,18},{3,19},{4,20},{5,21},{6,22},{7,23},{8,24},{9,... | collective-permute-start | bytes 884744 | tf_op jit(solution)/shard_map/ppermute | solution.py:34
  33.0 5.1 %collective-permute-done.6.refs_2_ = bf16[8,144,128]{2,1,0:T(8,128)(2,1)S(1)} collective-permute-done((bf16[8,144,128]{2,1,0:T(8,128)(2,1)S(1)}, bf16[8,144,128]{2,1,0:T(8,128)(2,1)S(1)}, u32[]{:S(2)}, u32[]{:S(2)}) %collective-permute-start.6) | collective-permute-done | bytes 294944 | tf_op jit(solution)/shard_map/ppermute | solution.py:34
  40.8 2.3 %collective-permute-start.11 = (bf16[8,144,128]{2,1,0:T(8,128)(2,1)S(1)}, bf16[8,144,128]{2,1,0:T(8,128)(2,1)S(1)}, u32[]{:S(2)}, u32[]{:S(2)}) collective-permute-start(bf16[8,144,128]{2,1,0:T(8,128)(2,1)S(1)} %shard_map.116.refs_3_.refs_9_), channel_id=1, source_target_pairs={{0,3},{1,0},{2,1},{3,2},{4,7},{5,4},{6,5},{7,6},{8,11},{9,8},{10,9... | collective-permute-start | bytes 884744 | tf_op jit(solution)/shard_map/ppermute | solution.py:30
  45.3 7.4 %shard_map.118.refs_1_.refs_9_ = f32[256,1024]{1,0:T(8,128)S(1)} custom-call(s32[5]{0:T(128)S(1)} %stack.32.refs_0_, bf16[256,8192]{1,0:T(8,128)(2,1)S(1)} %get-tuple-element.56.refs_1_.refs_2_.refs_5_.refs_6_, bf16[8192,1024]{1,0:T(8,128)(2,1)} %refs_6_.3, bf16[8,144,128]{2,1,0:T(8,128)(2,1)S(1)} %shard_map.116.refs_3_.refs_9_, ...), custom_call_target="tpu_custom_call" | custom-call | flops 11000000512 | bytes 33000000 | tf_op jit(solution)/shard_map/pallas_call | solution.py:54
  53.1 2.5 %collective-permute-done.14.refs_5_.refs_2_.refs_8_ = bf16[256,1024]{1,0:T(8,128)(2,1)S(1)} collective-permute-done((bf16[256,1024]{1,0:T(8,128)(2,1)S(1)}, bf16[256,1024]{1,0:T(8,128)(2,1)S(1)}, u32[]{:S(2)}, u32[]{:S(2)}) %collective-permute-start.14) | collective-permute-done | bytes 524320 | tf_op jit(solution)/shard_map/ppermute | solution.py:30
  57.0 2.7 %collective-permute-start.15 = (bf16[256,128]{1,0:T(8,128)(2,1)S(1)}, bf16[256,128]{1,0:T(8,128)(2,1)S(1)}, u32[]{:S(2)}, u32[]{:S(2)}) collective-permute-start(bf16[256,128]{1,0:T(8,128)(2,1)S(1)} %get-tuple-element.69), channel_id=1, source_target_pairs={{0,12},{1,13},{2,14},{3,15},{4,0},{5,1},{6,2},{7,3},{8,4},{9,5},{1... | collective-permute-start | bytes 196616 | tf_op jit(solution)/shard_map/ppermute | solution.py:30
  61.0 2.2 %collective-permute-done.15.refs_3_.refs_2_ = bf16[256,128]{1,0:T(8,128)(2,1)S(1)} collective-permute-done((bf16[256,128]{1,0:T(8,128)(2,1)S(1)}, bf16[256,128]{1,0:T(8,128)(2,1)S(1)}, u32[]{:S(2)}, u32[]{:S(2)}) %collective-permute-start.15) | collective-permute-done | bytes 65568 | tf_op jit(solution)/shard_map/ppermute | solution.py:30
  66.5 2.5 %collective-permute-done.19.refs_7_.refs_3_ = bf16[256,128]{1,0:T(8,128)(2,1)S(1)} collective-permute-done((bf16[256,128]{1,0:T(8,128)(2,1)S(1)}, bf16[256,128]{1,0:T(8,128)(2,1)S(1)}, u32[]{:S(2)}, u32[]{:S(2)}) %collective-permute-start.19) | collective-permute-done | bytes 65568 | tf_op jit(solution)/shard_map/ppermute | solution.py:30
  69.0 2.6 %collective-permute-done.20.refs_8_.refs_4_ = bf16[256,128]{1,0:T(8,128)(2,1)S(1)} collective-permute-done((bf16[256,128]{1,0:T(8,128)(2,1)S(1)}, bf16[256,128]{1,0:T(8,128)(2,1)S(1)}, u32[]{:S(2)}, u32[]{:S(2)}) %collective-permute-start.20) | collective-permute-done | bytes 65568 | tf_op jit(solution)/shard_map/ppermute | solution.py:30
  72.3 3.9 %collective-permute-start.26 = (bf16[8,144,128]{2,1,0:T(8,128)(2,1)S(1)}, bf16[8,144,128]{2,1,0:T(8,128)(2,1)S(1)}, u32[]{:S(2)}, u32[]{:S(2)}) collective-permute-start(bf16[8,144,128]{2,1,0:T(8,128)(2,1)S(1)} %shard_map.121.refs_2_.refs_9_), channel_id=1, source_target_pairs={{0,8},{1,9},{2,10},{3,11},{4,12},{5,13},{6,14},{7,15},{8,0},{9,1},... | collective-permute-start | bytes 884744 | tf_op jit(solution)/shard_map/ppermute | solution.py:30
  78.3 8.6 %shard_map.123 = (bf16[1296,128]{1,0:T(8,128)(2,1)S(1)}, bf16[1296,128]{1,0:T(8,128)(2,1)S(1)}, bf16[1296,128]{1,0:T(8,128)(2,1)S(1)}, bf16[1296,128]{1,0:T(8,128)(2,1)S(1)}) custom-call(s32[5]{0:T(128)S(1)} %stack.32.refs_0_, bf16[256,128]{1,0:T(8,128)(2,1)S(1)} %get-tuple-element.68.refs_4_.refs_1_, ...), custom_call_target="tpu_custom_call" | custom-call | flops 8499999744 | bytes 25500000 | tf_op jit(solution)/shard_map/pallas_call | solution.py:54
  87.5 3.5 %collective-permute-start.23 = (bf16[1296,128]{1,0:T(8,128)(2,1)S(1)}, bf16[1296,128]{1,0:T(8,128)(2,1)S(1)}, u32[]{:S(2)}, u32[]{:S(2)}) collective-permute-start(bf16[1296,128]{1,0:T(8,128)(2,1)S(1)} %get-tuple-element.77), channel_id=1, source_target_pairs={{0,8},{1,9},{2,10},{3,11},{4,12},{5,13},{6,14},{7,15},{8,0},{9,1},... | collective-permute-start | bytes 995336 | tf_op jit(solution)/shard_map/ppermute | solution.py:30
  91.1 8.6 %shard_map.124 = (bf16[1296,128]{1,0:T(8,128)(2,1)S(1)}, bf16[1296,128]{1,0:T(8,128)(2,1)S(1)}, bf16[1296,128]{1,0:T(8,128)(2,1)S(1)}, bf16[1296,128]{1,0:T(8,128)(2,1)S(1)}) custom-call(s32[5]{0:T(128)S(1)} %stack.32.refs_0_, bf16[256,128]{1,0:T(8,128)(2,1)S(1)} %get-tuple-element.79.refs_1_, bf16[256,128]{1,0:T(8,128)(2,1)S(1)} %collective-permute-done.18.refs_6_.refs_2_, ...), custom_call_target="tpu_custom_call" | custom-call | flops 8499999744 | bytes 25500000 | tf_op jit(solution)/shard_map/pallas_call | solution.py:54
  103.8 6.8 %shard_map.125 = (bf16[528,512]{1,0:T(8,128)(2,1)S(1)}, bf16[528,512]{1,0:T(8,128)(2,1)}, bf16[528,512]{1,0:T(8,128)(2,1)}, f32[512,512]{1,0:T(8,128)S(1)}, f32[1,512]{1,0:T(1,128)S(1)}) custom-call(s32[5]{0:T(128)S(1)} %stack.32.refs_0_, bf16[1296,128]{1,0:T(8,128)(2,1)S(1)} %get-tuple-element.75.refs_14_.refs_1_, ...), custom_call_target="tpu_custom_call" | custom-call | flops 6000000000 | bytes 18000000 | tf_op jit(solution)/shard_map/pallas_call | solution.py:54
  112.7 3.5 %collective-permute-done.30.refs_8_.refs_4_ = bf16[1296,128]{1,0:T(8,128)(2,1)S(1)} collective-permute-done((bf16[1296,128]{1,0:T(8,128)(2,1)S(1)}, bf16[1296,128]{1,0:T(8,128)(2,1)S(1)}, u32[]{:S(2)}, u32[]{:S(2)}) %collective-permute-start.30) | collective-permute-done | bytes 331808 | tf_op jit(solution)/shard_map/ppermute | solution.py:30
  116.2 5.6 %shard_map.126 = (bf16[256,4096]{1,0:T(8,128)(2,1)S(1)}, f32[256,128]{1,0:T(8,128)S(1)}, bf16[256,1024]{1,0:T(8,128)(2,1)S(1)}) custom-call(s32[5]{0:T(128)S(1)} %stack.32.refs_0_, bf16[1296,128]{1,0:T(8,128)(2,1)S(1)} %get-tuple-element.75.refs_14_.refs_1_, bf16[1296,128]{1,0:T(8,128)(2,1)S(1)} %collective-permute-done.22.refs_2_, ...), custom_call_target="tpu_custom_call" | custom-call | flops 8000000000 | bytes 24000000 | tf_op jit(solution)/shard_map/pallas_call | solution.py:54
  126.2 2.3 %collective-permute-done.36.refs_10_ = bf16[3,256,1024]{2,1,0:T(8,128)(2,1)S(1)} collective-permute-done((bf16[3,256,1024]{2,1,0:T(8,128)(2,1)S(1)}, bf16[3,256,1024]{2,1,0:T(8,128)(2,1)S(1)}, u32[]{:S(2)}, u32[]{:S(2)}) %collective-permute-start.36) | collective-permute-done | bytes 1572896 | tf_op jit(solution)/shard_map/ppermute | solution.py:38
  128.4 5.8 %shard_map.128 = (bf16[528,512]{1,0:T(8,128)(2,1)S(1)}, bf16[528,512]{1,0:T(8,128)(2,1)S(1)}, bf16[528,512]{1,0:T(8,128)(2,1)S(1)}, f32[512,512]{1,0:T(8,128)S(1)}, f32[1,512]{1,0:T(1,128)S(1)}) custom-call(s32[5]{0:T(128)S(1)} %stack.32.refs_0_, bf16[1296,128]{1,0:T(8,128)(2,1)S(1)} %get-tuple-element.80.refs_11_.refs_5_.refs_4_.refs_1_, ...), custom_call_target="tpu_custom_call" | custom-call | flops 100000000 | bytes 300000 | tf_op jit(solution)/shard_map/pallas_call | solution.py:54
  135.9 3.7 %shard_map.129.refs_6_ = bf16[256,2048]{1,0:T(8,128)(2,1)S(1)} custom-call(s32[5]{0:T(128)S(1)} %stack.32.refs_0_, bf16[256,1024]{1,0:T(8,128)(2,1)S(1)} %get-tuple-element.86.refs_1_, f32[256,128]{1,0:T(8,128)S(1)} %get-tuple-element.87.refs_2_, f32[256,128]{1,0:T(8,128)S(1)} %get-tuple-element.84.refs_10_.refs_3_, bf16[256,8192]{1,0:T(8,128)(2,1)S(1)} %copy-done.1, ...), custom_call_target="tpu_custom_call" | custom-call | flops 100000000 | bytes 300000 | tf_op jit(solution)/shard_map/pallas_call | solution.py:54
  141.7 2.2 %collective-permute-start.40 = (bf16[528,512]{1,0:T(8,128)(2,1)S(1)}, bf16[528,512]{1,0:T(8,128)(2,1)S(1)}, u32[]{:S(2)}, u32[]{:S(2)}) collective-permute-start(bf16[528,512]{1,0:T(8,128)(2,1)S(1)} %copy-done.12), channel_id=1, source_target_pairs={{0,8},{1,9},{2,10},{3,11},{4,12},{5,13},{6,14},{7,15},{8,0},{9,1},... | collective-permute-start | bytes 1622024 | tf_op jit(solution)/shard_map/ppermute | solution.py:30
  144.9 4.0 %collective-permute-done.34.refs_5_ = bf16[528,512]{1,0:T(8,128)(2,1)S(1)} collective-permute-done((bf16[528,512]{1,0:T(8,128)(2,1)}, bf16[528,512]{1,0:T(8,128)(2,1)S(1)}, u32[]{:S(2)}, u32[]{:S(2)}) %collective-permute-start.34) | collective-permute-done | bytes 540704 | tf_op jit(solution)/shard_map/ppermute | solution.py:30
  148.8 8.1 %collective-permute-done.32.refs_3_ = bf16[528,512]{1,0:T(8,128)(2,1)S(1)} collective-permute-done((bf16[528,512]{1,0:T(8,128)(2,1)S(1)}, bf16[528,512]{1,0:T(8,128)(2,1)S(1)}, u32[]{:S(2)}, u32[]{:S(2)}) %collective-permute-start.32) | collective-permute-done | bytes 540704 | tf_op jit(solution)/shard_map/ppermute | solution.py:30
  158.0 3.6 %collective-permute-start.38 = (bf16[272,512]{1,0:T(8,128)(2,1)S(1)}, bf16[272,512]{1,0:T(8,128)(2,1)S(1)}, u32[]{:S(2)}, u32[]{:S(2)}) collective-permute-start(bf16[272,512]{1,0:T(8,128)(2,1)S(1)} %get-tuple-element.96), channel_id=1, source_target_pairs={{0,16},{1,17},{2,18},{3,19},{4,20},{5,21},{6,22},{7,23},{8,24},{9,... | collective-permute-start | bytes 835592 | tf_op jit(solution)/shard_map/ppermute | solution.py:34
  161.6 3.7 %shard_map.131.refs_9_.refs_1_ = f32[256,2048]{1,0:T(8,128)S(1)} custom-call(s32[5]{0:T(128)S(1)} %stack.32.refs_0_, bf16[256,1024]{1,0:T(8,128)(2,1)S(1)} %get-tuple-element.86.refs_1_, f32[256,128]{1,0:T(8,128)S(1)} %get-tuple-element.87.refs_2_, f32[256,128]{1,0:T(8,128)S(1)} %get-tuple-element.84.refs_10_.refs_3_, bf16[256,8192]{1,0:T(8,128)(2,1)S(1)} %copy-done.1, ...), custom_call_target="tpu_custom_call" | custom-call | flops 100000000 | bytes 300000 | tf_op jit(solution)/shard_map/pallas_call | solution.py:54
  166.9 2.4 %collective-permute-done.41.refs_5_ = bf16[528,512]{1,0:T(8,128)(2,1)S(1)} collective-permute-done((bf16[528,512]{1,0:T(8,128)(2,1)S(1)}, bf16[528,512]{1,0:T(8,128)(2,1)S(1)}, u32[]{:S(2)}, u32[]{:S(2)}) %collective-permute-start.41) | collective-permute-done | bytes 540704 | tf_op jit(solution)/shard_map/ppermute | solution.py:30
  171.3 3.6 %collective-permute-start.42 = (bf16[272,512]{1,0:T(8,128)(2,1)S(1)}, bf16[272,512]{1,0:T(8,128)(2,1)S(1)}, u32[]{:S(2)}, u32[]{:S(2)}) collective-permute-start(bf16[272,512]{1,0:T(8,128)(2,1)S(1)} %get-tuple-element.103), channel_id=1, source_target_pairs={{0,16},{1,17},{2,18},{3,19},{4,20},{5,21},{6,22},{7,23},{8,24},{9,... | collective-permute-start | bytes 835592 | tf_op jit(solution)/shard_map/ppermute | solution.py:34
  176.8 4.7 %collective-permute-done.42.refs_7_ = bf16[272,512]{1,0:T(8,128)(2,1)S(1)} collective-permute-done((bf16[272,512]{1,0:T(8,128)(2,1)S(1)}, bf16[272,512]{1,0:T(8,128)(2,1)S(1)}, u32[]{:S(2)}, u32[]{:S(2)}) %collective-permute-start.42) | collective-permute-done | bytes 278560 | tf_op jit(solution)/shard_map/ppermute | solution.py:34
  (119 shorter events, 54.3 us)
Async XLA Ops:
  8.8 11.1 %collective-permute-start.1 = (bf16[416,128]{1,0:T(8,128)(2,1)S(1)}, bf16[416,128]{1,0:T(8,128)(2,1)S(1)}, u32[]{:S(2)}, u32[]{:S(2)}) collective-permute-start(bf16[416,128]{1,0:T(8,128)(2,1)S(1)} %get-tuple-element.58), channel_id=1, source_target_pairs={{0,8},{1,9},{2,10},{3,11},{4,12},{5,13},{6,14},{7,15},{8,0},{9,1},... | collective-permute-start | bytes 319496 | tf_op jit(solution)/shard_map/ppermute | solution.py:30
  9.6 10.3 %collective-permute-start.2 = (bf16[416,128]{1,0:T(8,128)(2,1)S(1)}, bf16[416,128]{1,0:T(8,128)(2,1)S(1)}, u32[]{:S(2)}, u32[]{:S(2)}) collective-permute-start(bf16[416,128]{1,0:T(8,128)(2,1)S(1)} %get-tuple-element.59), channel_id=1, source_target_pairs={{0,4},{1,5},{2,6},{3,7},{4,8},{5,9},{6,10},{7,11},{8,12},{9,13},{1... | collective-permute-start | bytes 319496 | tf_op jit(solution)/shard_map/ppermute | solution.py:30
  10.5 9.4 %collective-permute-start.3 = (bf16[416,128]{1,0:T(8,128)(2,1)S(1)}, bf16[416,128]{1,0:T(8,128)(2,1)S(1)}, u32[]{:S(2)}, u32[]{:S(2)}) collective-permute-start(bf16[416,128]{1,0:T(8,128)(2,1)S(1)} %get-tuple-element.61), channel_id=1, source_target_pairs={{0,3},{1,0},{2,1},{3,2},{4,7},{5,4},{6,5},{7,6},{8,11},{9,8},{10,9... | collective-permute-start | bytes 319496 | tf_op jit(solution)/shard_map/ppermute | solution.py:30
  22.0 17.1 %collective-permute-start.7 = (bf16[256,1024]{1,0:T(8,128)(2,1)S(1)}, bf16[256,1024]{1,0:T(8,128)(2,1)S(1)}, u32[]{:S(2)}, u32[]{:S(2)}) collective-permute-start(bf16[256,1024]{1,0:T(8,128)(2,1)S(1)} %get-tuple-element.64.refs_3_), channel_id=1, source_target_pairs={{0,12},{1,13},{2,14},{3,15},{4,0},{5,1},{6,2},{7,3},{8,4},{9,5},{1... | collective-permute-start | bytes 1572872 | tf_op jit(solution)/shard_map/ppermute | solution.py:30
  24.7 16.1 %collective-permute-start.8 = (bf16[256,1024]{1,0:T(8,128)(2,1)S(1)}, bf16[256,1024]{1,0:T(8,128)(2,1)S(1)}, u32[]{:S(2)}, u32[]{:S(2)}) collective-permute-start(bf16[256,1024]{1,0:T(8,128)(2,1)S(1)} %get-tuple-element.65.refs_4_), channel_id=1, source_target_pairs={{0,4},{1,5},{2,6},{3,7},{4,8},{5,9},{6,10},{7,11},{8,12},{9,13},{1... | collective-permute-start | bytes 1572872 | tf_op jit(solution)/shard_map/ppermute | solution.py:30
  25.9 17.2 %collective-permute-start.10 = (bf16[256,1024]{1,0:T(8,128)(2,1)S(1)}, bf16[256,1024]{1,0:T(8,128)(2,1)S(1)}, u32[]{:S(2)}, u32[]{:S(2)}) collective-permute-start(bf16[256,1024]{1,0:T(8,128)(2,1)S(1)} %get-tuple-element.67), channel_id=1, source_target_pairs={{0,1},{1,2},{2,3},{3,0},{4,5},{5,6},{6,7},{7,4},{8,9},{9,10},{10,1... | collective-permute-start | bytes 1572872 | tf_op jit(solution)/shard_map/ppermute | solution.py:30
  27.4 15.7 %collective-permute-start.9 = (bf16[256,1024]{1,0:T(8,128)(2,1)S(1)}, bf16[256,1024]{1,0:T(8,128)(2,1)S(1)}, u32[]{:S(2)}, u32[]{:S(2)}) collective-permute-start(bf16[256,1024]{1,0:T(8,128)(2,1)S(1)} %get-tuple-element.66.refs_3_), channel_id=1, source_target_pairs={{0,3},{1,0},{2,1},{3,2},{4,7},{5,4},{6,5},{7,6},{8,11},{9,8},{10,9... | collective-permute-start | bytes 1572872 | tf_op jit(solution)/shard_map/ppermute | solution.py:30
  38.7 14.0 %collective-permute-start.13 = (bf16[8,144,128]{2,1,0:T(8,128)(2,1)S(1)}, bf16[8,144,128]{2,1,0:T(8,128)(2,1)S(1)}, u32[]{:S(2)}, u32[]{:S(2)}) collective-permute-start(bf16[8,144,128]{2,1,0:T(8,128)(2,1)S(1)} %shard_map.116.refs_3_.refs_9_), channel_id=1, source_target_pairs={{0,1},{1,2},{2,3},{3,0},{4,5},{5,6},{6,7},{7,4},{8,9},{9,10},{10,1... | collective-permute-start | bytes 884744 | tf_op jit(solution)/shard_map/ppermute | solution.py:30
  39.1 13.6 %collective-permute-start.12 = (bf16[8,144,128]{2,1,0:T(8,128)(2,1)S(1)}, bf16[8,144,128]{2,1,0:T(8,128)(2,1)S(1)}, u32[]{:S(2)}, u32[]{:S(2)}) collective-permute-start(bf16[8,144,128]{2,1,0:T(8,128)(2,1)S(1)} %shard_map.116.refs_3_.refs_9_), channel_id=1, source_target_pairs={{0,2},{1,3},{2,0},{3,1},{4,6},{5,7},{6,4},{7,5},{8,10},{9,11},{10,... | collective-permute-start | bytes 884744 | tf_op jit(solution)/shard_map/ppermute | solution.py:30
  40.8 12.3 %collective-permute-start.11 = (bf16[8,144,128]{2,1,0:T(8,128)(2,1)S(1)}, bf16[8,144,128]{2,1,0:T(8,128)(2,1)S(1)}, u32[]{:S(2)}, u32[]{:S(2)}) collective-permute-start(bf16[8,144,128]{2,1,0:T(8,128)(2,1)S(1)} %shard_map.116.refs_3_.refs_9_), channel_id=1, source_target_pairs={{0,3},{1,0},{2,1},{3,2},{4,7},{5,4},{6,5},{7,6},{8,11},{9,8},{10,9... | collective-permute-start | bytes 884744 | tf_op jit(solution)/shard_map/ppermute | solution.py:30
  43.7 11.9 %collective-permute-start.14 = (bf16[256,1024]{1,0:T(8,128)(2,1)S(1)}, bf16[256,1024]{1,0:T(8,128)(2,1)S(1)}, u32[]{:S(2)}, u32[]{:S(2)}) collective-permute-start(bf16[256,1024]{1,0:T(8,128)(2,1)S(1)} %shard_map.117.refs_4_), channel_id=1, source_target_pairs={{0,8},{1,9},{2,10},{3,11},{4,12},{5,13},{6,14},{7,15},{8,0},{9,1},... | collective-permute-start | bytes 1572872 | tf_op jit(solution)/shard_map/ppermute | solution.py:30
  56.9 14.7 %collective-permute-start.21 = (bf16[3,256,1024]{2,1,0:T(8,128)(2,1)S(1)}, bf16[3,256,1024]{2,1,0:T(8,128)(2,1)S(1)}, u32[]{:S(2)}, u32[]{:S(2)}) collective-permute-start(bf16[3,256,1024]{2,1,0:T(8,128)(2,1)S(1)} %shard_map.120), channel_id=1, source_target_pairs={{0,32},{32,0},{64,96},{96,64},{1,33},{33,1},{65,97},{97,65},{2,34}... | collective-permute-start | bytes 4718600 | tf_op jit(solution)/shard_map/ppermute | solution.py:38
  72.2 15.3 %collective-permute-start.27 = (bf16[8,144,128]{2,1,0:T(8,128)(2,1)S(1)}, bf16[8,144,128]{2,1,0:T(8,128)(2,1)S(1)}, u32[]{:S(2)}, u32[]{:S(2)}) collective-permute-start(bf16[8,144,128]{2,1,0:T(8,128)(2,1)S(1)} %shard_map.121.refs_2_.refs_9_), channel_id=1, source_target_pairs={{0,4},{1,5},{2,6},{3,7},{4,8},{5,9},{6,10},{7,11},{8,12},{9,13},{1... | collective-permute-start | bytes 884744 | tf_op jit(solution)/shard_map/ppermute | solution.py:30
  72.3 18.8 %collective-permute-start.26 = (bf16[8,144,128]{2,1,0:T(8,128)(2,1)S(1)}, bf16[8,144,128]{2,1,0:T(8,128)(2,1)S(1)}, u32[]{:S(2)}, u32[]{:S(2)}) collective-permute-start(bf16[8,144,128]{2,1,0:T(8,128)(2,1)S(1)} %shard_map.121.refs_2_.refs_9_), channel_id=1, source_target_pairs={{0,8},{1,9},{2,10},{3,11},{4,12},{5,13},{6,14},{7,15},{8,0},{9,1},... | collective-permute-start | bytes 884744 | tf_op jit(solution)/shard_map/ppermute | solution.py:30
  76.2 14.9 %collective-permute-start.25 = (bf16[8,144,128]{2,1,0:T(8,128)(2,1)S(1)}, bf16[8,144,128]{2,1,0:T(8,128)(2,1)S(1)}, u32[]{:S(2)}, u32[]{:S(2)}) collective-permute-start(bf16[8,144,128]{2,1,0:T(8,128)(2,1)S(1)} %shard_map.121.refs_2_.refs_9_), channel_id=1, source_target_pairs={{0,12},{1,13},{2,14},{3,15},{4,0},{5,1},{6,2},{7,3},{8,4},{9,5},{1... | collective-permute-start | bytes 884744 | tf_op jit(solution)/shard_map/ppermute | solution.py:30
  77.0 45.0 %collective-permute-start.35 = (bf16[256,1024]{1,0:T(8,128)(2,1)S(1)}, bf16[256,1024]{1,0:T(8,128)(2,1)S(1)}, u32[]{:S(2)}, u32[]{:S(2)}) collective-permute-start(bf16[256,1024]{1,0:T(8,128)(2,1)S(1)} %shard_map.122.refs_14_), channel_id=1, source_target_pairs={{0,2},{1,3},{2,0},{3,1},{4,6},{5,7},{6,4},{7,5},{8,10},{9,11},{10,... | collective-permute-start | bytes 1572872 | tf_op jit(solution)/shard_map/ppermute | solution.py:30
  86.9 14.0 %collective-permute-start.22 = (bf16[1296,128]{1,0:T(8,128)(2,1)S(1)}, bf16[1296,128]{1,0:T(8,128)(2,1)S(1)}, u32[]{:S(2)}, u32[]{:S(2)}) collective-permute-start(bf16[1296,128]{1,0:T(8,128)(2,1)S(1)} %get-tuple-element.76), channel_id=1, source_target_pairs={{0,12},{1,13},{2,14},{3,15},{4,0},{5,1},{6,2},{7,3},{8,4},{9,5},{1... | collective-permute-start | bytes 995336 | tf_op jit(solution)/shard_map/ppermute | solution.py:30
  87.5 14.6 %collective-permute-start.23 = (bf16[1296,128]{1,0:T(8,128)(2,1)S(1)}, bf16[1296,128]{1,0:T(8,128)(2,1)S(1)}, u32[]{:S(2)}, u32[]{:S(2)}) collective-permute-start(bf16[1296,128]{1,0:T(8,128)(2,1)S(1)} %get-tuple-element.77), channel_id=1, source_target_pairs={{0,8},{1,9},{2,10},{3,11},{4,12},{5,13},{6,14},{7,15},{8,0},{9,1},... | collective-permute-start | bytes 995336 | tf_op jit(solution)/shard_map/ppermute | solution.py:30
  91.1 12.8 %collective-permute-start.24 = (bf16[1296,128]{1,0:T(8,128)(2,1)S(1)}, bf16[1296,128]{1,0:T(8,128)(2,1)S(1)}, u32[]{:S(2)}, u32[]{:S(2)}) collective-permute-start(bf16[1296,128]{1,0:T(8,128)(2,1)S(1)} %get-tuple-element.78), channel_id=1, source_target_pairs={{0,4},{1,5},{2,6},{3,7},{4,8},{5,9},{6,10},{7,11},{8,12},{9,13},{1... | collective-permute-start | bytes 995336 | tf_op jit(solution)/shard_map/ppermute | solution.py:30
  99.6 10.9 %collective-permute-start.28 = (bf16[1296,128]{1,0:T(8,128)(2,1)S(1)}, bf16[1296,128]{1,0:T(8,128)(2,1)S(1)}, u32[]{:S(2)}, u32[]{:S(2)}) collective-permute-start(bf16[1296,128]{1,0:T(8,128)(2,1)S(1)} %get-tuple-element.81), channel_id=1, source_target_pairs={{0,3},{1,0},{2,1},{3,2},{4,7},{5,4},{6,5},{7,6},{8,11},{9,8},{10,9... | collective-permute-start | bytes 995336 | tf_op jit(solution)/shard_map/ppermute | solution.py:30
  100.9 11.8 %collective-permute-start.29 = (bf16[1296,128]{1,0:T(8,128)(2,1)S(1)}, bf16[1296,128]{1,0:T(8,128)(2,1)S(1)}, u32[]{:S(2)}, u32[]{:S(2)}) collective-permute-start(bf16[1296,128]{1,0:T(8,128)(2,1)S(1)} %get-tuple-element.82), channel_id=1, source_target_pairs={{0,2},{1,3},{2,0},{3,1},{4,6},{5,7},{6,4},{7,5},{8,10},{9,11},{10,... | collective-permute-start | bytes 995336 | tf_op jit(solution)/shard_map/ppermute | solution.py:30
  102.1 14.0 %collective-permute-start.30 = (bf16[1296,128]{1,0:T(8,128)(2,1)S(1)}, bf16[1296,128]{1,0:T(8,128)(2,1)S(1)}, u32[]{:S(2)}, u32[]{:S(2)}) collective-permute-start(bf16[1296,128]{1,0:T(8,128)(2,1)S(1)} %get-tuple-element.83), channel_id=1, source_target_pairs={{0,1},{1,2},{2,3},{3,0},{4,5},{5,6},{6,7},{7,4},{8,9},{9,10},{10,1... | collective-permute-start | bytes 995336 | tf_op jit(solution)/shard_map/ppermute | solution.py:30
  121.7 14.2 %collective-permute-start.31 = (bf16[256,4096]{1,0:T(8,128)(2,1)S(1)}, bf16[256,4096]{1,0:T(8,128)(2,1)S(1)}, u32[]{:S(2)}, u32[]{:S(2)}) collective-permute-start(bf16[256,4096]{1,0:T(8,128)(2,1)S(1)} %get-tuple-element.88.refs_11_), channel_id=1, source_target_pairs={{0,32},{32,0},{64,96},{96,64},{1,33},{33,1},{65,97},{97,65},{2,34}... | collective-permute-start | bytes 6291464 | tf_op jit(solution)/shard_map/ppermute | solution.py:38
  123.3 20.7 %collective-permute-start.33 = (bf16[528,512]{1,0:T(8,128)(2,1)}, bf16[528,512]{1,0:T(8,128)(2,1)S(1)}, u32[]{:S(2)}, u32[]{:S(2)}) collective-permute-start(bf16[528,512]{1,0:T(8,128)(2,1)} %get-tuple-element.91), channel_id=1, source_target_pairs={{0,2},{1,3},{2,0},{3,1},{4,6},{5,7},{6,4},{7,5},{8,10},{9,11},{10,... | collective-permute-start | bytes 1622024 | tf_op jit(solution)/shard_map/ppermute | solution.py:30
  124.9 23.9 %collective-permute-start.34 = (bf16[528,512]{1,0:T(8,128)(2,1)}, bf16[528,512]{1,0:T(8,128)(2,1)S(1)}, u32[]{:S(2)}, u32[]{:S(2)}) collective-permute-start(bf16[528,512]{1,0:T(8,128)(2,1)} %get-tuple-element.92), channel_id=1, source_target_pairs={{0,3},{1,0},{2,1},{3,2},{4,7},{5,4},{6,5},{7,6},{8,11},{9,8},{10,9... | collective-permute-start | bytes 1622024 | tf_op jit(solution)/shard_map/ppermute | solution.py:30
  139.7 35.3 %collective-permute-start.37 = (bf16[256,2048]{1,0:T(8,128)(2,1)S(1)}, bf16[256,2048]{1,0:T(8,128)(2,1)S(1)}, u32[]{:S(2)}, u32[]{:S(2)}) collective-permute-start(bf16[256,2048]{1,0:T(8,128)(2,1)S(1)} %shard_map.129.refs_6_), channel_id=1, source_target_pairs={{0,64},{32,96},{64,0},{96,32},{1,65},{33,97},{65,1},{97,33},{2,66}... | collective-permute-start | bytes 3145736 | tf_op jit(solution)/shard_map/ppermute | solution.py:38
  141.7 15.3 %collective-permute-start.32 = (bf16[528,512]{1,0:T(8,128)(2,1)S(1)}, bf16[528,512]{1,0:T(8,128)(2,1)S(1)}, u32[]{:S(2)}, u32[]{:S(2)}) collective-permute-start(bf16[528,512]{1,0:T(8,128)(2,1)S(1)} %copy-done.8), channel_id=1, source_target_pairs={{0,1},{1,2},{2,3},{3,0},{4,5},{5,6},{6,7},{7,4},{8,9},{9,10},{10,1... | collective-permute-start | bytes 1622024 | tf_op jit(solution)/shard_map/ppermute | solution.py:30
  141.7 25.1 %collective-permute-start.40 = (bf16[528,512]{1,0:T(8,128)(2,1)S(1)}, bf16[528,512]{1,0:T(8,128)(2,1)S(1)}, u32[]{:S(2)}, u32[]{:S(2)}) collective-permute-start(bf16[528,512]{1,0:T(8,128)(2,1)S(1)} %copy-done.12), channel_id=1, source_target_pairs={{0,8},{1,9},{2,10},{3,11},{4,12},{5,13},{6,14},{7,15},{8,0},{9,1},... | collective-permute-start | bytes 1622024 | tf_op jit(solution)/shard_map/ppermute | solution.py:30
  144.0 25.3 %collective-permute-start.41 = (bf16[528,512]{1,0:T(8,128)(2,1)S(1)}, bf16[528,512]{1,0:T(8,128)(2,1)S(1)}, u32[]{:S(2)}, u32[]{:S(2)}) collective-permute-start(bf16[528,512]{1,0:T(8,128)(2,1)S(1)} %copy-done.10), channel_id=1, source_target_pairs={{0,12},{1,13},{2,14},{3,15},{4,0},{5,1},{6,2},{7,3},{8,4},{9,5},{1... | collective-permute-start | bytes 1622024 | tf_op jit(solution)/shard_map/ppermute | solution.py:30
  148.8 20.4 %collective-permute-start.39 = (bf16[528,512]{1,0:T(8,128)(2,1)S(1)}, bf16[528,512]{1,0:T(8,128)(2,1)S(1)}, u32[]{:S(2)}, u32[]{:S(2)}) collective-permute-start(bf16[528,512]{1,0:T(8,128)(2,1)S(1)} %get-tuple-element.93.refs_7_), channel_id=1, source_target_pairs={{0,4},{1,5},{2,6},{3,7},{4,8},{5,9},{6,10},{7,11},{8,12},{9,13},{1... | collective-permute-start | bytes 1622024 | tf_op jit(solution)/shard_map/ppermute | solution.py:30
  158.0 18.8 %collective-permute-start.38 = (bf16[272,512]{1,0:T(8,128)(2,1)S(1)}, bf16[272,512]{1,0:T(8,128)(2,1)S(1)}, u32[]{:S(2)}, u32[]{:S(2)}) collective-permute-start(bf16[272,512]{1,0:T(8,128)(2,1)S(1)} %get-tuple-element.96), channel_id=1, source_target_pairs={{0,16},{1,17},{2,18},{3,19},{4,20},{5,21},{6,22},{7,23},{8,24},{9,... | collective-permute-start | bytes 835592 | tf_op jit(solution)/shard_map/ppermute | solution.py:34
  171.3 10.1 %collective-permute-start.42 = (bf16[272,512]{1,0:T(8,128)(2,1)S(1)}, bf16[272,512]{1,0:T(8,128)(2,1)S(1)}, u32[]{:S(2)}, u32[]{:S(2)}) collective-permute-start(bf16[272,512]{1,0:T(8,128)(2,1)S(1)} %get-tuple-element.103), channel_id=1, source_target_pairs={{0,16},{1,17},{2,18},{3,19},{4,20},{5,21},{6,22},{7,23},{8,24},{9,... | collective-permute-start | bytes 835592 | tf_op jit(solution)/shard_map/ppermute | solution.py:34
  (27 other events, 146.9 us)
